TPU v7x, 32 devices: a whole 2x2x4 slice. The times are simulated.
32 devices in a mesh: slab: 8 (over z, y), chan: 4 (over x, core).
Axes of the slice: x: 2, y: 2, z: 4, core: 2. Of those that a mesh axis runs over, the one named last changes fastest.
Arguments:
- field: bfloat16 [64, 256, 4096], P(None, 'slab'), may hold values from -6 to 6
- cotangent: bfloat16 [64, 256, 4096], P(None, 'slab'), may hold values from -10 to 10
- spectral_weight: bfloat16 [2, 64, 64, 512, 32], P(None, 'chan', None, 'slab'), may hold values from -4 to 4
- point_weight: bfloat16 [64, 64], replicated, may hold values from -0.75 to 0.75
- point_bias: bfloat16 [64], replicated, may hold values from -2 to 2
Outputs:
- grad_input: bfloat16 [64, 256, 4096], P('chan', 'slab')
- grad_spectral: float32 [2, 64, 64, 512, 32], P(None, 'chan', None, 'slab')
- grad_pointwise: float32 [64, 64], P('chan')
- grad_bias: float32 [64], replicated
All inputs are finite; a program needn't handle non-finite values.
Results may differ from a plain program's by a relative error of at most 0.023.
Values may be sent and summed in bfloat16 or wider, within the bound.
A program may use at most 256 MiB of HBM per device.

v0:
```python
import math

import jax
import jax.numpy as jnp
from jax import lax
from jax.sharding import PartitionSpec as P

MX = 32
MY = 32
MZ = 16
NX = 256
NY = 64
NZ = 64


def kept_modes(total, length):
    mode_index = jnp.arange(total, dtype=jnp.int32)
    return jnp.where(mode_index < total // 2, mode_index, mode_index - total + length)


def phases(frequency, length):
    positions = jnp.arange(length, dtype=jnp.int32)
    wound_up = frequency[:, None] * positions[None, :] % length
    return 2.0 * math.pi / length * wound_up.astype(jnp.float32)


def make_tables():
    angle_z = phases(jnp.arange(MZ, dtype=jnp.int32), NZ)
    cosine_z = jnp.cos(angle_z)
    sine_z = jnp.sin(angle_z)
    forward_z = jnp.stack([cosine_z.T, -sine_z.T], 1).astype(jnp.bfloat16)
    weight_z = (jnp.where(jnp.arange(MZ) == 0, 1.0, 2.0) / (NX * NY * NZ)).astype(jnp.float32)
    scaled_z = jnp.stack([weight_z[:, None] * cosine_z, -weight_z[:, None] * sine_z], 1).astype(
        jnp.bfloat16
    )
    plain_z = jnp.stack([cosine_z, -sine_z], 1).astype(jnp.bfloat16)
    angle_y = phases(kept_modes(MY, NY), NY)
    cosine_y = jnp.cos(angle_y)
    sine_y = jnp.sin(angle_y)
    upper_rows = jnp.stack([cosine_y.T, -sine_y.T], -1)
    lower_rows = jnp.stack([sine_y.T, cosine_y.T], -1)
    forward_y = jnp.stack([upper_rows, lower_rows], 0).reshape(2 * NY, 2 * MY).astype(jnp.bfloat16)
    real_rows = jnp.stack([cosine_y, sine_y], 1)
    imag_rows = jnp.stack([-sine_y, cosine_y], 1)
    inverse_y = jnp.stack([real_rows, imag_rows], 1).reshape(2 * MY, 2 * NY).astype(jnp.bfloat16)
    angle_x = phases(kept_modes(MX, NX), NX)
    cosine_x = jnp.cos(angle_x).T.astype(jnp.bfloat16)
    sine_x = jnp.sin(angle_x).T.astype(jnp.bfloat16)
    return (forward_z, scaled_z, plain_z, forward_y, inverse_y, cosine_x, sine_x)


def to_modes(field_part, tables):
    forward_z, scaled_z, plain_z, forward_y, inverse_y, cosine_x, sine_x = tables
    channels = field_part.shape[0]
    planes = field_part.shape[1]
    grid_view = field_part.reshape(channels, planes, NY, NZ)
    section_one = jnp.einsum(
        "cxyz,zpk->cxkpy", grid_view, forward_z, preferred_element_type=jnp.float32
    ).astype(jnp.bfloat16)
    section_one = section_one.reshape(channels, planes, MZ, 2 * NY)
    section_two = jnp.einsum(
        "cxkm,mn->cxkn", section_one, forward_y, preferred_element_type=jnp.float32
    ).astype(jnp.bfloat16)
    section_two = section_two.reshape(channels, planes, 2 * MZ * MY)
    pencils = lax.all_to_all(section_two, "slab", split_axis=2, concat_axis=1, tiled=True)
    pencils = pencils.reshape(channels, NX, -1, 2)
    along_cos = jnp.einsum("cxmq,xk->cmqk", pencils, cosine_x, preferred_element_type=jnp.float32)
    along_sin = jnp.einsum("cxmq,xk->cmqk", pencils, sine_x, preferred_element_type=jnp.float32)
    real_part = along_cos[:, :, 0] + along_sin[:, :, 1]
    imag_part = along_cos[:, :, 1] - along_sin[:, :, 0]
    return jnp.stack([real_part, imag_part], 2)


def to_grid(spectra, tables, table_z):
    forward_z, scaled_z, plain_z, forward_y, inverse_y, cosine_x, sine_x = tables
    channels = spectra.shape[0]
    back_cos = jnp.einsum("cmqk,xk->cxmq", spectra, cosine_x, preferred_element_type=jnp.float32)
    back_sin = jnp.einsum("cmqk,xk->cxmq", spectra, sine_x, preferred_element_type=jnp.float32)
    real_part = back_cos[..., 0] - back_sin[..., 1]
    imag_part = back_cos[..., 1] + back_sin[..., 0]
    pencil_rows = jnp.stack([real_part, imag_part], -1).astype(jnp.bfloat16)
    pencil_rows = pencil_rows.reshape(channels, NX, -1)
    slabs = lax.all_to_all(pencil_rows, "slab", split_axis=1, concat_axis=2, tiled=True)
    channels = slabs.shape[0]
    planes = slabs.shape[1]
    slabs = slabs.reshape(channels, planes, MZ, 2 * MY)
    section_two = jnp.einsum(
        "cxkn,nm->cxkm", slabs, inverse_y, preferred_element_type=jnp.float32
    ).astype(jnp.bfloat16)
    section_two = section_two.reshape(channels, planes, MZ, 2, NY)
    grid_view = jnp.einsum(
        "cxkpy,kpz->cxyz", section_two, table_z, preferred_element_type=jnp.float32
    )
    return grid_view.reshape(channels, planes, NY * NZ)


def gelu_grad(pre_act):
    normal_cdf = 0.5 * (1.0 + jax.scipy.special.erf(pre_act / math.sqrt(2.0)))
    normal_pdf = jnp.exp(-0.5 * pre_act * pre_act) / math.sqrt(2.0 * math.pi)
    return normal_cdf + pre_act * normal_pdf


def body(field, cotangent, spectral_weight, point_weight, point_bias):
    tables = make_tables()
    scaled_z = tables[1]
    plain_z = tables[2]
    group_size = spectral_weight.shape[1]
    modes_dev = spectral_weight.shape[3]
    chan_start = lax.axis_index("chan") * group_size
    own_field = lax.dynamic_slice_in_dim(field, chan_start, group_size, 0)
    coeff = to_modes(own_field, tables).astype(jnp.bfloat16)
    coeff_real = coeff[:, :, 0]
    coeff_imag = coeff[:, :, 1]
    real_weight = spectral_weight[0]
    imag_weight = spectral_weight[1]
    spec_real = jnp.einsum(
        "imk,iomk->omk", coeff_real, real_weight, preferred_element_type=jnp.float32
    ) - jnp.einsum("imk,iomk->omk", coeff_imag, imag_weight, preferred_element_type=jnp.float32)
    spec_imag = jnp.einsum(
        "imk,iomk->omk", coeff_real, imag_weight, preferred_element_type=jnp.float32
    ) + jnp.einsum("imk,iomk->omk", coeff_imag, real_weight, preferred_element_type=jnp.float32)
    partial_spectra = jnp.stack([spec_real, spec_imag], 2)
    spectra = lax.psum(partial_spectra.astype(jnp.bfloat16), "chan")
    shaped = to_grid(spectra, tables, scaled_z)
    mixed = jnp.einsum("io,ixc->oxc", point_weight, field, preferred_element_type=jnp.float32)
    pre_act = shaped + mixed + point_bias.astype(jnp.float32)[:, None, None]
    grad_pre = (cotangent.astype(jnp.float32) * gelu_grad(pre_act)).astype(jnp.bfloat16)
    mode_index = lax.axis_index("slab") * modes_dev + jnp.arange(modes_dev, dtype=jnp.int32)
    mode_scale = (jnp.where(mode_index // MY == 0, 1.0, 2.0) / (NX * NY * NZ)).astype(jnp.float32)
    grad_own = lax.dynamic_slice_in_dim(grad_pre, chan_start, group_size, 0)
    part_hat = (to_modes(grad_own, tables) * mode_scale[None, :, None, None]).astype(jnp.bfloat16)
    grad_hat = lax.all_gather(part_hat, "chan", axis=0, tiled=True)
    grad_real = grad_hat[:, :, 0]
    grad_imag = grad_hat[:, :, 1]
    outer_real = jnp.einsum(
        "imk,omk->iomk", coeff_real, grad_real, preferred_element_type=jnp.float32
    ) + jnp.einsum("imk,omk->iomk", coeff_imag, grad_imag, preferred_element_type=jnp.float32)
    outer_imag = jnp.einsum(
        "imk,omk->iomk", coeff_real, grad_imag, preferred_element_type=jnp.float32
    ) - jnp.einsum("imk,omk->iomk", coeff_imag, grad_real, preferred_element_type=jnp.float32)
    grad_spectral = jnp.stack([outer_real, outer_imag], 0)
    adj_real = jnp.einsum(
        "omk,iomk->imk", grad_real, real_weight, preferred_element_type=jnp.float32
    ) + jnp.einsum("omk,iomk->imk", grad_imag, imag_weight, preferred_element_type=jnp.float32)
    adj_imag = jnp.einsum(
        "omk,iomk->imk", grad_imag, real_weight, preferred_element_type=jnp.float32
    ) - jnp.einsum("omk,iomk->imk", grad_real, imag_weight, preferred_element_type=jnp.float32)
    adjoint = jnp.stack([adj_real, adj_imag], 2).astype(jnp.bfloat16)
    spectral_back = to_grid(adjoint, tables, plain_z)
    own_rows = lax.dynamic_slice_in_dim(point_weight, chan_start, group_size, 0)
    point_back = jnp.einsum("io,oxc->ixc", own_rows, grad_pre, preferred_element_type=jnp.float32)
    grad_input = (spectral_back + point_back).astype(jnp.bfloat16)
    inverse_root = 1.0 / math.sqrt(NX * NY * NZ)
    weight_part = (
        jnp.einsum("ixc,oxc->io", own_field, grad_pre, preferred_element_type=jnp.float32)
        * inverse_root
    )
    bias_part = jnp.sum(grad_pre, axis=(1, 2), dtype=jnp.float32) * inverse_root
    grad_pointwise, grad_bias = lax.psum((weight_part, bias_part), "slab")
    return (grad_input, grad_spectral, grad_pointwise, grad_bias)


def solution(mesh):
    placed = (
        P(None, "slab", None),
        P(None, "slab", None),
        P(None, "chan", None, "slab", None),
        P(),
        P(),
    )
    return jax.shard_map(
        body,
        mesh=mesh,
        in_specs=placed,
        out_specs=(
            P("chan", "slab", None),
            P(None, "chan", None, "slab", None),
            P("chan", None),
            P(),
        ),
        check_vma=False,
    )
```

profile of v0, /device:TPU:13, one launch (start us, length us, event | category | flops | bytes accessed | tf_op | source)
XLA Modules:
  0.0 766.6 jit_solution(10531408997758893496)
XLA Ops:
  7.6 18.5 %copy.172 = bf16[64,32,4096]{2,0,1:T(8,128)(2,1)} copy(bf16[64,32,4096]{2,1,0:T(8,128)(2,1)} %param.5) | data formatting | bytes 33554432 | tf_op args[0]
  34.9 12.7 %reshape.577 = bf16[16,32,64,64,1]{3,2,1,0,4:T(8,128)(2,1)} reshape(bf16[16,32,4096]{2,1,0:T(8,128)(2,1)} %copy.173) | data formatting | bytes 8388608 | tf_op jit(solution)/shard_map/reshape | solution.py:56
  47.7 11.2 %convert_bitcast_fusion.1 = bf16[16,32,16,2,64]{4,2,1,0,3:T(8,128)(2,1)S(1)} fusion(bf16[16,32,64,64,1]{3,2,1,0,4:T(8,128)(2,1)} %reshape.577, bf16[64,1,16]{0,2,1:T(8,128)(2,1)S(1)} %get-tuple-element.78, bf16[64,1,16]{0,2,1:T(8,128)(2,1)S(1)} %get-tuple-element.79), kind=kOutput, calls=%fused_computation.42 | convolution fusion | flops 135274496 | bytes 6295552 | tf_op jit(solution)/shard_map/cxyz,zpk->cxkpy/dot_general | solution.py:57
  95.8 23.2 %all-to-all-done = bf16[8,2,32768]{2,1,0:T(2,128)(2,1)S(1)} async-done(((bf16[8,2,32768]{2,1,0:T(2,128)(2,1)}), bf16[8,2,32768]{2,1,0:T(2,128)(2,1)S(1)}, u32[]{:S(2)}, u32[]{:S(2)}) %all-to-all-start) | async-done | bytes 1048608 | tf_op jit(solution)/shard_map/all_to_all | solution.py:65
  123.4 9.1 %copy.178 = bf16[16,8,32,128]{2,1,0,3:T(8,128)(2,1)} copy(bf16[16,8,32,128]{2,0,3,1:T(8,128)(2,1)} %bitcast.223) | data formatting | bytes 2097152 | tf_op jit(solution)/shard_map/all_to_all | solution.py:65
  140.6 11.2 %fusion.9 = (f32[64,32,64]{0,1,2:T(8,128)S(1)}, f32[64,32,64]{0,1,2:T(8,128)S(1)}, f32[64,32,64]{0,1,2:T(8,128)S(1)}, f32[64,32,64]{0,1,2:T(8,128)S(1)}) fusion(f32[64,32,16]{0,1,2:T(8,128)S(1)} %bitcast_convert_fusion.2, bf16[2,16,64,64,32]{3,4,2,1,0:T(8,128)(2,1)} %param.7, f32[64,32,16]{0,1,2:T(8,128)S(1)} %bitcast_convert_fusion.3), kind=kLoop, calls=%fused_computation.22 | loop fusion | flops 20447232 | bytes 10747904 | tf_op jit(solution)/shard_map/imk,iomk->omk/dot_general | solution.py:118
  153.4 37.4 %all-reduce.3.cloned.1.call-done = bf16[64,64,2,32]{1,3,2,0:T(8,128)(2,1)} async-done(((bf16[64,64,2,32]{1,3,2,0:T(8,128)(2,1)}), bf16[64,64,2,32]{1,3,2,0:T(8,128)(2,1)}) %all-reduce.3.cloned.1.call-update) | async-done | bytes 524304 | tf_op jit(solution)/shard_map/psum | solution.py:123
  215.2 90.1 %all-to-all-done.1 = bf16[64,256,128]{2,0,1:T(8,128)(2,1)} async-done(((bf16[64,256,128]{2,0,1:T(8,128)(2,1)}), bf16[64,256,128]{2,0,1:T(8,128)(2,1)}, u32[]{:S(2)}, u32[]{:S(2)}) %all-to-all-start.1) | async-done | bytes 4194336 | tf_op jit(solution)/shard_map/all_to_all | solution.py:83
  312.2 11.0 %reshape.566 = bf16[64,32,16,64]{3,2,1,0:T(8,128)(2,1)} reshape(bf16[64,32,8,128]{3,2,1,0:T(8,128)(2,1)} %copy.184) | data formatting | bytes 8388608 | tf_op jit(solution)/shard_map/reshape | solution.py:86
  332.1 27.8 %reshape.567 = bf16[64,32,16,2,64]{4,3,2,1,0:T(2,128)(2,1)} reshape(bf16[64,32,16,128]{3,2,1,0:T(8,128)(2,1)} %convolution_convert_fusion) | data formatting | bytes 16777216 | tf_op jit(solution)/shard_map/reshape | solution.py:90
  359.9 28.8 %convolution_bitcast_fusion = f32[64,32,64,64]{3,2,1,0:T(8,128)} fusion(bf16[64,32,16,2,64]{4,3,2,1,0:T(2,128)(2,1)} %reshape.567, bf16[16,1,64]{2,0,1:T(8,128)(2,1)S(1)} %multiply_convert_fusion, bf16[16,1,64]{2,0,1:T(8,128)(2,1)S(1)} %multiply_convert_fusion.1), kind=kOutput, calls=%fused_computation.11 | convolution fusion | flops 536872960 | bytes 41947136 | tf_op jit(solution)/shard_map/cxkpy,kpz->cxyz/dot_general | solution.py:91
  388.8 54.7 %reshape.568 = f32[64,32,4096]{2,1,0:T(8,128)} reshape(f32[64,32,64,64]{3,2,1,0:T(8,128)} %convolution_bitcast_fusion) | data formatting | bytes 67108864 | tf_op jit(solution)/shard_map/reshape | solution.py:94
  443.5 81.2 %convert_reduce_fusion = (f32[64]{0:T(128)S(1)}, bf16[64,32,4096]{2,0,1:T(8,128)(2,1)S(1)}) fusion(f32[64]{0:T(128)S(1)} %convert_element_type.232, bf16[64,32,4096]{2,1,0:T(8,128)(2,1)} %param.5, bf16[64,64]{1,0:T(8,128)(2,1)S(1)} %copy-done, f32[64,32,4096]{2,1,0:T(8,128)} %reshape.568, bf16[64,32,4096]{2,1,0:T(8,128)(2,1)} %param.6), kind=kOutput, calls=%fused_computation.10 | convolution fusion | flops 1199570944 | bytes 83894784 | tf_op jit(solution)/shard_map/io,ixc->oxc/dot_general | solution.py:125
  535.3 12.7 %reshape.593 = bf16[16,32,64,64,1]{3,2,1,0,4:T(8,128)(2,1)} reshape(bf16[16,32,4096]{2,1,0:T(8,128)(2,1)} %copy.190) | data formatting | bytes 8388608 | tf_op jit(solution)/shard_map/reshape | solution.py:56
  548.0 11.2 %convert_bitcast_fusion = bf16[16,32,16,2,64]{4,2,1,0,3:T(8,128)(2,1)S(1)} fusion(bf16[16,32,64,64,1]{3,2,1,0,4:T(8,128)(2,1)} %reshape.593, bf16[64,1,16]{0,2,1:T(8,128)(2,1)S(1)} %copy-done.10, bf16[64,1,16]{0,2,1:T(8,128)(2,1)S(1)} %copy-done.12), kind=kOutput, calls=%fused_computation.41 | convolution fusion | flops 135274496 | bytes 6295552 | tf_op jit(solution)/shard_map/cxyz,zpk->cxkpy/dot_general | solution.py:57
  596.8 11.5 %fusion.20 = f32[16,64]{1,0:T(8,128)S(1)} fusion(bf16[16,32,4096]{2,0,1:T(8,128)(2,1)} %copy-done.2, bf16[64,32,4096]{2,0,1:T(8,128)(2,1)} %copy-done.1), kind=kOutput, calls=%fused_computation.51 | convolution fusion | flops 268436480 | bytes 20975616 | tf_op jit(solution)/shard_map/ixc,oxc->io/dot_general | solution.py:155
  608.2 20.8 %all-reduce = (f32[16,64]{1,0:T(8,128)}, f32[64]{0:T(128)}) all-reduce(f32[16,64]{1,0:T(8,128)S(1)} %fusion.20, f32[64]{0:T(128)S(1)} %broadcast_multiply_fusion), channel_id=1, replica_groups=mesh['slab'=8,'chan'=4] {'slab'}, use_global_device_ids=true, to_apply=%region_1.2 | all-reduce | flops 1088 | bytes 8704 | tf_op jit(solution)/shard_map/psum | solution.py:159
  633.5 9.1 %copy.194 = bf16[16,8,32,128]{2,1,0,3:T(8,128)(2,1)} copy(bf16[16,8,32,128]{2,0,3,1:T(8,128)(2,1)} %bitcast.224) | data formatting | bytes 2097152 | tf_op jit(solution)/shard_map/all_to_all | solution.py:65
  649.9 12.3 %all_gather.3 = bf16[64,64,2,32]{1,3,2,0:T(8,128)(2,1)S(1)} all-gather(bf16[16,64,2,32]{1,3,2,0:T(8,128)(2,1)S(1)} %fusion.33), channel_id=1, replica_groups=mesh['slab'=8,'chan'=4] {'chan'}, dimensions={0}, use_global_device_ids=true | all-gather | bytes 655360 | tf_op jit(solution)/shard_map/all_gather | solution.py:132
  662.8 11.9 %fusion.13 = (f32[64,32,16]{0,1,2:T(8,128)S(1)}, f32[64,32,16]{0,1,2:T(8,128)S(1)}, f32[64,32,16]{0,1,2:T(8,128)S(1)}, f32[64,32,16]{0,1,2:T(8,128)S(1)}) fusion(f32[64,32,64]{0,1,2:T(8,128)S(1)} %get-tuple-element.58, bf16[2,16,64,64,32]{3,4,2,1,0:T(8,128)(2,1)} %param.7, f32[64,32,64]{0,1,2:T(8,128)S(1)} %get-tuple-element.57), kind=kLoop, calls=%fused_computation.26 | loop fusion | flops 20840448 | bytes 9961472 | tf_op jit(solution)/shard_map/omk,iomk->imk/dot_general | solution.py:144
  690.4 11.9 %pad_maximum_fusion = f32[2,16,64,64,32]{3,4,2,1,0:T(8,128)} fusion(f32[1,16,64,64,32]{3,4,2,1,0:T(8,128)S(1)} %get-tuple-element.55, f32[1,16,64,64,32]{3,4,2,1,0:T(8,128)S(1)} %get-tuple-element.54), kind=kLoop, calls=%fused_computation.7 | loop fusion | flops 4194304 | bytes 33554432 | tf_op jit(solution)/shard_map/stack | solution.py:141
  715.7 10.3 %convolution_bitcast_fusion.1 = f32[16,32,64,64]{3,2,1,0:T(8,128)} fusion(bf16[16,32,16,2,64]{4,3,2,1,0:T(2,128)(2,1)} %reshape.574, bf16[16,1,64]{2,0,1:T(8,128)(2,1)S(1)} %get-tuple-element.80, bf16[16,1,64]{2,0,1:T(8,128)(2,1)S(1)} %get-tuple-element.81), kind=kOutput, calls=%fused_computation.31 | convolution fusion | flops 134219776 | bytes 10489856 | tf_op jit(solution)/shard_map/cxkpy,kpz->cxyz/dot_general | solution.py:91
  726.0 14.9 %reshape.575 = f32[16,32,4096]{2,1,0:T(8,128)} reshape(f32[16,32,64,64]{3,2,1,0:T(8,128)} %convolution_bitcast_fusion.1) | data formatting | bytes 16777216 | tf_op jit(solution)/shard_map/reshape | solution.py:94
  740.9 14.3 %fusion.16 = bf16[16,32,4096]{2,0,1:T(8,128)(2,1)S(1)} fusion(f32[16,32,4096]{2,1,0:T(8,128)} %reshape.575, bf16[64,32,4096]{2,0,1:T(8,128)(2,1)} %copy-done.1, bf16[64,64]{1,0:T(8,128)(2,1)S(1)} %copy-done, s32[]{:T(128)S(6)} %select_n.204), kind=kOutput, calls=%fused_computation.33 | convolution fusion | flops 272629760 | bytes 29364228 | tf_op jit(solution)/shard_map/io,oxc->ixc/dot_general | solution.py:151
  (113 shorter events, 194.0 us)
Async XLA Ops:
  7.2 436.4 %copy-start = (bf16[64,64]{1,0:T(8,128)(2,1)S(1)}, bf16[64,64]{1,0:T(8,128)(2,1)}, u32[]{:S(2)}) copy-start(bf16[64,64]{1,0:T(8,128)(2,1)} %param.8) | copy-start | bytes 24580
  7.3 40.4 %copy-start.9 = (bf16[64,1,16]{0,2,1:T(8,128)(2,1)}, bf16[64,1,16]{0,2,1:T(8,128)(2,1)S(1)}, u32[]{:S(2)}) copy-start(bf16[64,1,16]{0,2,1:T(8,128)(2,1)S(1)} %get-tuple-element.78) | copy-start | bytes 6148
  7.3 40.4 %copy-start.11 = (bf16[64,1,16]{0,2,1:T(8,128)(2,1)}, bf16[64,1,16]{0,2,1:T(8,128)(2,1)S(1)}, u32[]{:S(2)}) copy-start(bf16[64,1,16]{0,2,1:T(8,128)(2,1)S(1)} %get-tuple-element.79) | copy-start | bytes 6148
  7.6 67.0 %copy-start.5 = (bf16[128,64,1,1]{0,1,2,3:T(8,128)(2,1)}, bf16[128,64,1,1]{0,1,2,3:T(8,128)(2,1)S(1)}, u32[]{:S(2)}) copy-start(bf16[128,64,1,1]{0,1,2,3:T(8,128)(2,1)S(1)} %reshape.578) | copy-start | bytes 49156
  28.6 2.0 copy-start.2
  90.1 28.9 %all-to-all-start = ((bf16[8,2,32768]{2,1,0:T(2,128)(2,1)}), bf16[8,2,32768]{2,1,0:T(2,128)(2,1)S(1)}, u32[]{:S(2)}, u32[]{:S(2)}) async-start(bf16[8,2,32768]{2,1,0:T(2,128)(2,1)} %reshape.610), calls=%async_computation | async-start | bytes 2097152 | tf_op jit(solution)/shard_map/all_to_all | solution.py:65
  95.7 95.1 %all-reduce.3.cloned.1.call-start = ((), (), s32[]{:S(2)}) async-start(), calls=%async_computation.4 | async-start | bytes 2097152 | tf_op jit(solution)/shard_map/psum | solution.py:123
  95.7 97.8 %copy-start.13 = (s32[32]{0:T(128)}, s32[32]{0:T(128)S(1)}, u32[]{:S(2)}) copy-start(s32[32]{0:T(128)S(1)} %compare_select_fusion.1) | copy-start | bytes 388
  190.8 2.8 copy-start.3
  201.6 13.4 %copy-start.15 = (bf16[64]{0:T(256)(128)(2,1)S(1)}, bf16[64]{0:T(256)(128)(2,1)}, u32[]{:S(2)}) copy-start(bf16[64]{0:T(256)(128)(2,1)} %param.9) | copy-start | bytes 388
  209.0 96.3 %all-to-all-start.1 = ((bf16[64,256,128]{2,0,1:T(8,128)(2,1)}), bf16[64,256,128]{2,0,1:T(8,128)(2,1)}, u32[]{:S(2)}, u32[]{:S(2)}) async-start(bf16[64,256,128]{2,0,1:T(8,128)(2,1)} %copy.182), calls=%async_computation.1 | async-start | bytes 8388608 | tf_op jit(solution)/shard_map/all_to_all | solution.py:83
  215.0 108.2 %copy-start.7 = (bf16[64,128,1,1]{1,0,2,3:T(8,128)(2,1)}, bf16[64,128,1,1]{1,0,2,3:T(8,128)(2,1)S(1)}, u32[]{:S(2)}) copy-start(bf16[64,128,1,1]{1,0,2,3:T(8,128)(2,1)S(1)} %reshape.589) | copy-start | bytes 49156
  524.7 5.8 copy-start.1
  535.2 12.7 %copy-start.10 = (bf16[64,1,16]{0,2,1:T(8,128)(2,1)S(1)}, bf16[64,1,16]{0,2,1:T(8,128)(2,1)}, u32[]{:S(2)}) copy-start(bf16[64,1,16]{0,2,1:T(8,128)(2,1)} %copy-done.9) | copy-start | bytes 6148
  535.3 12.7 %copy-start.12 = (bf16[64,1,16]{0,2,1:T(8,128)(2,1)S(1)}, bf16[64,1,16]{0,2,1:T(8,128)(2,1)}, u32[]{:S(2)}) copy-start(bf16[64,1,16]{0,2,1:T(8,128)(2,1)} %copy-done.11) | copy-start | bytes 6148
  559.2 15.5 %copy-start.6 = (bf16[128,64,1,1]{0,1,2,3:T(8,128)(2,1)S(1)}, bf16[128,64,1,1]{0,1,2,3:T(8,128)(2,1)}, u32[]{:S(2)}) copy-start(bf16[128,64,1,1]{0,1,2,3:T(8,128)(2,1)} %copy-done.5) | copy-start | bytes 49156
  590.2 38.9 %all-to-all-start.2 = ((bf16[8,2,32768]{2,1,0:T(2,128)(2,1)}), bf16[8,2,32768]{2,1,0:T(2,128)(2,1)S(1)}, u32[]{:S(2)}, u32[]{:S(2)}) async-start(bf16[8,2,32768]{2,1,0:T(2,128)(2,1)} %reshape.612), calls=%async_computation.2 | async-start | bytes 2097152 | tf_op jit(solution)/shard_map/all_to_all | solution.py:65
  629.1 18.9 %copy-start.14 = (s32[32]{0:T(128)S(1)}, s32[32]{0:T(128)}, u32[]{:S(2)}) copy-start(s32[32]{0:T(128)} %copy-done.13) | copy-start | bytes 388
  675.4 9.0 %copy-start.4 = (f32[64,32,16]{0,1,2:T(8,128)S(1)}, f32[64,32,16]{0,1,2:T(8,128)}, u32[]{:S(2)}) copy-start(f32[64,32,16]{0,1,2:T(8,128)} %get-tuple-element.46) | copy-start | bytes 393220
  679.7 28.0 %all-to-all-start.3 = ((bf16[16,256,128]{2,0,1:T(8,128)(2,1)}), bf16[16,256,128]{2,0,1:T(8,128)(2,1)S(1)}, u32[]{:S(2)}, u32[]{:S(2)}) async-start(bf16[16,256,128]{2,0,1:T(8,128)(2,1)} %copy.198), calls=%async_computation.3 | async-start | bytes 2097152 | tf_op jit(solution)/shard_map/all_to_all | solution.py:83
  690.4 19.7 %copy-start.8 = (bf16[64,128,1,1]{1,0,2,3:T(8,128)(2,1)S(1)}, bf16[64,128,1,1]{1,0,2,3:T(8,128)(2,1)}, u32[]{:S(2)}) copy-start(bf16[64,128,1,1]{1,0,2,3:T(8,128)(2,1)} %copy-done.7) | copy-start | bytes 49156
Sparse Core Ops, SparseCore 0:
  153.6 37.2 all-reduce.2
where the time goes:
time: 780 us; the launch traced here: 767 us
  local copies, waits for them, and re-layouts  300 us (38%)
  matrix products  193 us (25%)
  waiting for transfers between devices  156 us (20%)
  other arithmetic  47.7 us (6%)
  blocking collectives  33.2 us (4%)
  starting transfers between devices  22.6 us (3%)
  between operations  14.8 us (2%)
    all_to_all x2, waiting for transfers between devices, to_grid(): lax.all_to_all(pencil_rows, 'slab', split_axis=1, concat_axis=2, tiled=True)  95.4 us
    dot_general x1, matrix products, body(): jnp.einsum('io,ixc->oxc', point_weight, field, preferred_element_type=jnp...  81.2 us
    reshape x2, local copies, waits for them, and re-layouts, to_grid(): return grid_view.reshape(channels, planes, NY * NZ)  69.7 us
    unnamed x38, local copies, waits for them, and re-layouts  55.2 us
    dot_general x2, matrix products, to_grid(): jnp.einsum('cxkpy,kpz->cxyz', section_two, table_z, preferred_element_typ...  39.2 us
    psum x1, waiting for transfers between devices, body(): spectra = lax.psum(partial_spectra.astype(jnp.bfloat16), 'chan')  37.4 us
    reshape x2, local copies, waits for them, and re-layouts, to_grid(): section_two = section_two.reshape(channels, planes, MZ, 2, NY)  31.1 us
    reshape x2, local copies, waits for them, and re-layouts, to_modes(): grid_view = field_part.reshape(channels, planes, NY, NZ)  25.4 us
  transfers between devices with their start and end apart: 5, of which 4 were waited for; matrix products, arithmetic and copies ran while one was open for 4% of the time, Pallas kernels for 0%

commit v1 on v0

v1 whole, which is shorter than its diff:
```python
import functools
import math

import jax
import jax.numpy as jnp
import ml_dtypes
import numpy as np
from jax import lax
from jax.experimental import pallas as pl
from jax.experimental.pallas import tpu as pltpu
from jax.sharding import PartitionSpec as P

MX = 32
MY = 32
MZ = 16
NY = 64
NZ = 64

BF16 = ml_dtypes.bfloat16
VMEM_LIMIT = 50 * 1024 * 1024


def kept_modes(total, length):
    mode_index = np.arange(total, dtype=np.int32)
    return np.where(mode_index < total // 2, mode_index, mode_index - total + length)


def rounded_waves(frequency, length):
    positions = np.arange(length, dtype=np.int32)
    wound_up = frequency[:, None] * positions[None, :] % length
    angle = np.float32(2.0 * math.pi / length) * wound_up.astype(np.float32)
    cosine = np.cos(angle).astype(BF16).astype(np.float32)
    sine = np.sin(angle).astype(BF16).astype(np.float32)
    return cosine, sine


def plane_table(slabs):
    cosine_z, sine_z = rounded_waves(np.arange(MZ, dtype=np.int32), NZ)
    cosine_y, sine_y = rounded_waves(kept_modes(MY, NY), NY)
    cz, sz = cosine_z.T[None, :, :, None], sine_z.T[None, :, :, None]
    cy, sy = cosine_y.T[:, None, None, :], sine_y.T[:, None, None, :]
    real = (cz * cy - sz * sy).reshape(NY * NZ, slabs, 1, -1)
    imag = -(cz * sy + sz * cy).reshape(NY * NZ, slabs, 1, -1)
    return np.concatenate([real, imag], 2).reshape(NY * NZ, -1).astype(BF16)


def line_tables(length):
    cosine, sine = rounded_waves(kept_modes(MX, length), length)
    return cosine.astype(BF16), sine.astype(BF16)


def gelu_grad(pre_act):
    normal_cdf = 0.5 * (1.0 + lax.erf(pre_act * (1.0 / math.sqrt(2.0))))
    normal_pdf = jnp.exp(-0.5 * pre_act * pre_act) * (1.0 / math.sqrt(2.0 * math.pi))
    return normal_cdf + pre_act * normal_pdf


def params():
    return pltpu.CompilerParams(vmem_limit_bytes=VMEM_LIMIT)


def pick(total, wanted):
    return math.gcd(total, wanted)


def mix_kernel(coeff_ref, weight_ref, out_ref, *, inner):
    group, outs = weight_ref.shape[1], weight_ref.shape[2]
    shape = weight_ref.shape[3:]

    def some_outputs(step, carry):
        first = step * inner

        def one_input(i, sums):
            real, imag = coeff_ref[i, 0], coeff_ref[i, 1]
            done = []
            for k in range(inner):
                wr = weight_ref[0, i, first + k].astype(jnp.float32)
                wi = weight_ref[1, i, first + k].astype(jnp.float32)
                done.append(sums[2 * k] + (real * wr - imag * wi))
                done.append(sums[2 * k + 1] + (real * wi + imag * wr))
            return tuple(done)

        zero = jnp.zeros(shape, jnp.float32)
        sums = lax.fori_loop(0, group, one_input, (zero,) * (2 * inner), unroll=2)
        for k in range(inner):
            out_ref[first + k, 0] = sums[2 * k].astype(out_ref.dtype)
            out_ref[first + k, 1] = sums[2 * k + 1].astype(out_ref.dtype)
        return carry

    lax.fori_loop(0, outs // inner, some_outputs, 0)


def mix(coeff, weight):
    group, channels, lines, modes = weight.shape[1:]
    block = pick(channels, 8)
    return pl.pallas_call(
        functools.partial(mix_kernel, inner=pick(block, 4)),
        grid=(channels // block,),
        in_specs=[
            pl.BlockSpec((group, 2, lines, modes), lambda s: (0, 0, 0, 0)),
            pl.BlockSpec((2, group, block, lines, modes), lambda s: (0, 0, s, 0, 0)),
        ],
        out_specs=pl.BlockSpec((block, 2, lines, modes), lambda s: (s, 0, 0, 0)),
        out_shape=jax.ShapeDtypeStruct((channels, 2, lines, modes), jnp.bfloat16),
        compiler_params=params(),
        cost_estimate=pl.CostEstimate(
            flops=8 * weight.size // 2, bytes_accessed=4 * weight.size, transcendentals=0
        ),
        name="mix",
    )(coeff, weight)


def adjoint_kernel(hat_ref, weight_ref, out_ref, *, inner):
    own, channels = weight_ref.shape[1], weight_ref.shape[2]
    shape = weight_ref.shape[3:]
    for first in range(0, own, inner):

        def one_output(o, sums):
            real, imag = hat_ref[o, 0], hat_ref[o, 1]
            done = []
            for k in range(inner):
                wr = weight_ref[0, first + k, o].astype(jnp.float32)
                wi = weight_ref[1, first + k, o].astype(jnp.float32)
                done.append(sums[2 * k] + (real * wr + imag * wi))
                done.append(sums[2 * k + 1] + (imag * wr - real * wi))
            return tuple(done)

        zero = jnp.zeros(shape, jnp.float32)
        sums = lax.fori_loop(0, channels, one_output, (zero,) * (2 * inner), unroll=2)
        for k in range(inner):
            out_ref[first + k, 0] = sums[2 * k].astype(out_ref.dtype)
            out_ref[first + k, 1] = sums[2 * k + 1].astype(out_ref.dtype)


def adjoint_of(hat, weight):
    group, channels, lines, modes = weight.shape[1:]
    block = pick(group, 2)
    return pl.pallas_call(
        functools.partial(adjoint_kernel, inner=block),
        grid=(group // block,),
        in_specs=[
            pl.BlockSpec((channels, 2, lines, modes), lambda s: (0, 0, 0, 0)),
            pl.BlockSpec((2, block, channels, lines, modes), lambda s: (0, s, 0, 0, 0)),
        ],
        out_specs=pl.BlockSpec((block, 2, lines, modes), lambda s: (s, 0, 0, 0)),
        out_shape=jax.ShapeDtypeStruct((group, 2, lines, modes), jnp.bfloat16),
        compiler_params=params(),
        cost_estimate=pl.CostEstimate(
            flops=8 * weight.size // 2, bytes_accessed=4 * weight.size, transcendentals=0
        ),
        name="adjoint",
    )(hat, weight)


def outer_kernel(coeff_ref, hat_ref, out_ref):
    own, channels = out_ref.shape[1], out_ref.shape[2]
    for i in range(own):
        cr, ci = coeff_ref[i, 0], coeff_ref[i, 1]

        def one_output(o, carry):
            hr, hi = hat_ref[o, 0], hat_ref[o, 1]
            out_ref[0, i, o] = cr * hr + ci * hi
            out_ref[1, i, o] = cr * hi - ci * hr
            return carry

        lax.fori_loop(0, channels, one_output, 0, unroll=4)


def outer(coeff, hat):
    group, _, lines, modes = coeff.shape
    channels = hat.shape[0]
    block = pick(group, 2)
    return pl.pallas_call(
        outer_kernel,
        grid=(group // block,),
        in_specs=[
            pl.BlockSpec((block, 2, lines, modes), lambda s: (s, 0, 0, 0)),
            pl.BlockSpec((channels, 2, lines, modes), lambda s: (0, 0, 0, 0)),
        ],
        out_specs=pl.BlockSpec((2, block, channels, lines, modes), lambda s: (0, s, 0, 0, 0)),
        out_shape=jax.ShapeDtypeStruct((2, group, channels, lines, modes), jnp.float32),
        compiler_params=params(),
        cost_estimate=pl.CostEstimate(
            flops=6 * group * channels * lines * modes,
            bytes_accessed=16 * group * channels * lines * modes,
            transcendentals=0,
        ),
        name="outer",
    )(coeff, hat)


ROWS_BY_ROWS = (((1,), (1,)), ((), ()))


def grid_kernel(
    modes_ref, table_ref, field_ref, cotangent_ref, mix_ref, back_ref, bias_ref,
    point_ref, hat_ref, weight_ref, sum_ref, total,
):
    step = pl.program_id(0)

    @pl.when(step == 0)
    def _():
        total[...] = jnp.zeros_like(total)
        weight_ref[...] = jnp.zeros_like(weight_ref)
        sum_ref[...] = jnp.zeros_like(sum_ref)

    table = table_ref[...]
    field = field_ref[...]
    pre_act = lax.dot_general(
        modes_ref[...], table, ROWS_BY_ROWS, preferred_element_type=jnp.float32
    )
    pre_act += jnp.dot(mix_ref[...], field, preferred_element_type=jnp.float32)
    pre_act += bias_ref[...]
    grad_wide = cotangent_ref[...].astype(jnp.float32) * gelu_grad(pre_act)
    grad_pre = grad_wide.astype(jnp.bfloat16)
    point_ref[...] = jnp.dot(
        back_ref[...], grad_pre, preferred_element_type=jnp.float32
    ).astype(point_ref.dtype)
    total[...] += jnp.dot(grad_pre, table, preferred_element_type=jnp.float32)
    weight_ref[...] += lax.dot_general(
        field, grad_pre, ROWS_BY_ROWS, preferred_element_type=jnp.float32
    )
    sum_ref[...] += jnp.sum(grad_pre.astype(jnp.float32), axis=1, keepdims=True)

    @pl.when(step == pl.num_programs(0) - 1)
    def _():
        hat_ref[...] = total[...].astype(hat_ref.dtype)


def grid_stage(modes, table, field, cotangent, mixing, backing, bias):
    rows, width = modes.shape
    cells = table.shape[0]
    block = pick(cells, 512)
    still = lambda s: (0, 0)
    along = lambda s: (0, s)
    return pl.pallas_call(
        grid_kernel,
        grid=(cells // block,),
        in_specs=[
            pl.BlockSpec((rows, width), still),
            pl.BlockSpec((block, width), lambda s: (s, 0)),
            pl.BlockSpec((rows, block), along),
            pl.BlockSpec((rows, block), along),
            pl.BlockSpec((rows, rows), still),
            pl.BlockSpec((rows, rows), still),
            pl.BlockSpec((rows, 1), still),
        ],
        out_specs=[
            pl.BlockSpec((rows, block), along),
            pl.BlockSpec((rows, width), still),
            pl.BlockSpec((rows, rows), still),
            pl.BlockSpec((rows, 1), still),
        ],
        out_shape=[
            jax.ShapeDtypeStruct((rows, cells), jnp.bfloat16),
            jax.ShapeDtypeStruct((rows, width), jnp.bfloat16),
            jax.ShapeDtypeStruct((rows, rows), jnp.float32),
            jax.ShapeDtypeStruct((rows, 1), jnp.float32),
        ],
        scratch_shapes=[pltpu.VMEM((rows, width), jnp.float32)],
        compiler_params=params(),
        cost_estimate=pl.CostEstimate(
            flops=2 * rows * cells * (2 * width + 3 * rows),
            bytes_accessed=2 * cells * (width + 3 * rows),
            transcendentals=2 * rows * cells,
        ),
        name="grid",
    )(modes, table, field, cotangent, mixing, backing, bias)


def pad_planes(array, dim, spare):
    if not spare:
        return array
    return jnp.pad(array, [(0, spare if d == dim else 0) for d in range(array.ndim)])


def line_modes(pencils, tables):
    cosine, sine = tables
    along_cos = jnp.einsum("cxqm,kx->cqkm", pencils, cosine, preferred_element_type=jnp.float32)
    along_sin = jnp.einsum("cxqm,kx->cqkm", pencils, sine, preferred_element_type=jnp.float32)
    real = along_cos[:, 0] + along_sin[:, 1]
    imag = along_cos[:, 1] - along_sin[:, 0]
    return jnp.stack([real, imag], 1)


def line_values(spectra, tables):
    cosine, sine = tables
    back_cos = jnp.einsum("cqkm,kx->cxqm", spectra, cosine, preferred_element_type=jnp.float32)
    back_sin = jnp.einsum("cqkm,kx->cxqm", spectra, sine, preferred_element_type=jnp.float32)
    real = back_cos[:, :, 0] - back_sin[:, :, 1]
    imag = back_cos[:, :, 1] + back_sin[:, :, 0]
    return jnp.stack([real, imag], 2)


def body(slabs, chans, field, cotangent, spectral_weight, point_weight, point_bias):
    channels, planes, cells = field.shape
    group = spectral_weight.shape[1]
    modes = spectral_weight.shape[3]
    own_planes = -(-planes // chans)
    spare = own_planes * chans - planes
    length = planes * slabs
    width = 2 * modes
    table = lax.optimization_barrier(jnp.asarray(plane_table(slabs)))
    tables = tuple(jnp.asarray(t) for t in line_tables(length))
    slab_index = lax.axis_index("slab")
    chan_index = lax.axis_index("chan")
    weight = jnp.swapaxes(spectral_weight, 3, 4)
    scale = 1.0 / (length * cells)
    mode_index = slab_index * modes + jnp.arange(modes, dtype=jnp.int32)
    mode_scale = (jnp.where(mode_index // MY == 0, 1.0, 2.0) * scale).astype(jnp.float32)

    own_field = lax.dynamic_slice_in_dim(field, chan_index * group, group, 0)
    sections = jnp.einsum(
        "rc,csn->srn",
        own_field.reshape(group * planes, cells),
        table.reshape(cells, slabs, width),
        preferred_element_type=jnp.float32,
    ).astype(jnp.bfloat16)
    pencils = lax.all_to_all(sections, "slab", split_axis=0, concat_axis=0, tiled=True)
    pencils = pencils.reshape(slabs, group, planes, 2, modes)
    pencils = jnp.moveaxis(pencils, 1, 0).reshape(group, length, 2, modes)
    coeff = line_modes(pencils, tables).astype(jnp.bfloat16).astype(jnp.float32)

    partial = mix(coeff, weight)
    spectra = lax.psum_scatter(partial, "chan", scatter_dimension=0, tiled=True)
    pencils = line_values(spectra, tables) * mode_scale
    pencils = pencils.astype(jnp.bfloat16).reshape(group, slabs, planes, width)
    pencils = pad_planes(pencils, 2, spare).reshape(group, slabs, chans, own_planes, width)
    pencils = jnp.transpose(pencils, (1, 2, 0, 3, 4))
    pencils = pencils.reshape(slabs * chans, group, own_planes, width)
    slabs_in = lax.all_to_all(
        pencils, ("slab", "chan"), split_axis=0, concat_axis=0, tiled=True
    )
    slabs_in = slabs_in.reshape(slabs, channels, own_planes, width)
    rows = channels * own_planes
    slabs_in = jnp.transpose(slabs_in, (1, 2, 0, 3)).reshape(rows, slabs * width)

    first_plane = chan_index * own_planes
    plane_field = lax.dynamic_slice_in_dim(
        pad_planes(field, 1, spare), first_plane, own_planes, 1
    )
    plane_cotangent = lax.dynamic_slice_in_dim(
        pad_planes(cotangent, 1, spare), first_plane, own_planes, 1
    )
    eye = jnp.eye(own_planes, dtype=jnp.bfloat16)
    point, hat_rows, weight_part, bias_part = grid_stage(
        slabs_in,
        table,
        plane_field.reshape(rows, cells),
        plane_cotangent.reshape(rows, cells),
        jnp.kron(point_weight.T, eye),
        jnp.kron(point_weight, eye),
        jnp.repeat(point_bias.astype(jnp.float32), own_planes)[:, None],
    )
    point = lax.all_to_all(
        point.reshape(chans, group, own_planes, cells),
        "chan", split_axis=0, concat_axis=0, tiled=True,
    )
    hat_rows = hat_rows.reshape(chans, group, own_planes, slabs, width)
    hat_rows = jnp.transpose(hat_rows, (3, 0, 1, 2, 4))
    hat_rows = hat_rows.reshape(slabs * chans, group, own_planes, width)
    pencils = lax.all_to_all(
        hat_rows, ("slab", "chan"), split_axis=0, concat_axis=0, tiled=True
    )
    pencils = jnp.moveaxis(pencils.reshape(slabs, chans, group, own_planes, width), 2, 0)
    pencils = pencils.reshape(group, slabs, chans * own_planes, width)[:, :, :planes]
    pencils = pencils.reshape(group, length, 2, modes)
    part_hat = (line_modes(pencils, tables) * mode_scale).astype(jnp.bfloat16)
    hat = lax.all_gather(part_hat, "chan", axis=0, tiled=True).astype(jnp.float32)

    adjoint = adjoint_of(hat, weight)
    grad_spectral = jnp.swapaxes(outer(coeff, hat), 3, 4)
    pencils = line_values(adjoint, tables).astype(jnp.bfloat16)
    pencils = pencils.reshape(group, slabs, planes, width)
    pencils = lax.all_to_all(
        jnp.moveaxis(pencils, 1, 0), "slab", split_axis=0, concat_axis=0, tiled=True
    )
    pencils = jnp.moveaxis(pencils, 0, 2).reshape(group * planes, slabs * width)
    back = lax.dot_general(pencils, table, ROWS_BY_ROWS, preferred_element_type=jnp.float32)
    back = back.reshape(group, planes, cells)
    point = jnp.moveaxis(point, 0, 1).reshape(group, chans * own_planes, cells)[:, :planes]
    grad_input = (back + point.astype(jnp.float32)).astype(jnp.bfloat16)

    inverse_root = 1.0 / math.sqrt(length * cells)
    weight_part = weight_part.reshape(channels, own_planes, channels, own_planes)
    weight_part = jnp.einsum("ipop->io", weight_part)
    bias_part = bias_part.reshape(channels, own_planes).sum(1)
    sums = jnp.concatenate([weight_part, bias_part[None]], 0) * inverse_root
    sums = lax.psum(sums, ("slab", "chan"))
    grad_pointwise = lax.dynamic_slice_in_dim(sums, chan_index * group, group, 0)
    return (grad_input, grad_spectral, grad_pointwise, sums[channels])


def solution(mesh):
    placed = (
        P(None, "slab", None),
        P(None, "slab", None),
        P(None, "chan", None, "slab", None),
        P(),
        P(),
    )
    return jax.shard_map(
        functools.partial(body, mesh.shape["slab"], mesh.shape["chan"]),
        mesh=mesh,
        in_specs=placed,
        out_specs=(
            P("chan", "slab", None),
            P(None, "chan", None, "slab", None),
            P("chan", None),
            P(),
        ),
        check_vma=False,
    )
```

time: 780 us -> 392 us (0.50); the launches traced: 767 us -> 389 us
  local copies, waits for them, and re-layouts: 300 us -> 89.8 us
  matrix products: 193 us -> 21.9 us
  waiting for transfers between devices: 156 us -> 26.8 us
  blocking collectives: 33.2 us -> 144 us
  Pallas kernels: 0 us -> 58.4 us
  other arithmetic: 47.7 us -> 17.1 us
    dot_general x19 -> x10, matrix products: 193 us -> 21.9 us  [the longest x1 11.4 us: body(): lax.dot_general(pencils, table, ROWS_BY_ROWS, preferred_element_type=jnp....]
    reshape x14 -> x9, local copies, waits for them, and re-layouts: 175 us -> 27.7 us  [the longest x1 11.9 us: body(): weight_part.reshape(channels, own_planes, channels, own_planes)]
    all_to_all x4 -> x3, waiting for transfers between devices: 119 us -> 0.01 us  [the longest x1 0.01 us: body(): lax.all_to_all(point.reshape(chans, group, own_planes, cells), 'chan', sp...]
    pallas_call x0 -> x4, Pallas kernels: none -> 58.4 us  [the longest x1 23.5 us: grid_stage(): pl.pallas_call(grid_kernel, grid=(cells // block,), in_specs=[pl.BlockSpe...]
    all_to_all x0 -> x2, blocking collectives: none -> 57.5 us  [the longest x1 29.4 us: body(): lax.all_to_all(hat_rows, ('slab', 'chan'), split_axis=0, concat_axis=0, t...]
    unnamed x38 -> x12, local copies, waits for them, and re-layouts: 55.2 us -> 3.1 us
    psum x1 -> x0, waiting for transfers between devices: 37.4 us -> none  [body(): spectra = lax.psum(partial_spectra.astype(jnp.bfloat16), 'chan')]
    all_gather x1, blocking collectives: 12.3 us -> 46.6 us  [body(): lax.all_gather(part_hat, 'chan', axis=0, tiled=True).astype(jnp.float32)]
  transfers between devices with their start and end apart: 5 -> 4, of which waited for: 4 -> 1; matrix products, arithmetic and copies ran while one was open for 4% -> 22% of each run, Pallas kernels for 0% -> 6%
where the time goes in v1:
time: 392 us; the launch traced here: 389 us
  blocking collectives  144 us (37%)
  local copies, waits for them, and re-layouts  89.8 us (23%)
  Pallas kernels  58.4 us (15%)
  waiting for transfers between devices  26.8 us (7%)
  matrix products  21.9 us (6%)
  other arithmetic  17.1 us (4%)
  starting transfers between devices  17 us (4%)
  between operations  14.3 us (4%)
    all_gather x1, blocking collectives, body(): lax.all_gather(part_hat, 'chan', axis=0, tiled=True).astype(jnp.float32)  46.6 us
    psum x1, blocking collectives, body(): sums = lax.psum(sums, ('slab', 'chan'))  39.5 us
    all_to_all x1, blocking collectives, body(): lax.all_to_all(hat_rows, ('slab', 'chan'), split_axis=0, concat_axis=0, t...  29.4 us
    all_to_all x1, blocking collectives, body(): lax.all_to_all(sections, 'slab', split_axis=0, concat_axis=0, tiled=True)  28.2 us
    reduce_scatter x1, waiting for transfers between devices, body(): spectra = lax.psum_scatter(partial, 'chan', scatter_dimension=0, tiled=True)  26.8 us
    pallas_call x1, Pallas kernels, grid_stage(): pl.pallas_call(grid_kernel, grid=(cells // block,), in_specs=[pl.BlockSpe...  23.5 us
    another operation x3, local copies, waits for them, and re-layouts, line_values(): return jnp.stack([real, imag], 2)  14.6 us
    mul x1, local copies, waits for them, and re-layouts, body(): jnp.kron(point_weight.T, eye)  12.9 us
  transfers between devices with their start and end apart: 4, of which 1 were waited for; matrix products, arithmetic and copies ran while one was open for 22% of the time, Pallas kernels for 6%

profile of v1, /device:TPU:13, one launch (start us, length us, event | category | flops | bytes accessed | tf_op | source)
XLA Modules:
  0.0 388.9 jit_solution(15442070195085415533)
XLA Ops:
  11.9 4.6 %fusion.11 = bf16[8,512,128]{2,1,0:T(8,128)(2,1)S(1)} fusion(bf16[512,4096,1]{1,0,2:T(8,128)(2,1)S(1)} %bitcast.122, bf16[4096,1024]{1,0:T(8,128)(2,1)S(1)} %copy-done.5), kind=kOutput, calls=%fused_computation.20 | convolution fusion | flops 4295491584 | bytes 13631488 | tf_op jit(solution)/shard_map/rc,csn->srn/dot_general | solution.py:313
  16.4 28.2 %all_to_all.25 = bf16[8,512,128]{2,1,0:T(8,128)(2,1)} all-to-all(bf16[8,512,128]{2,1,0:T(8,128)(2,1)S(1)} %fusion.11), channel_id=1, replica_groups=mesh['slab'=8,'chan'=4] {'slab'}, dimensions={0} | all-to-all | bytes 2097152 | tf_op jit(solution)/shard_map/all_to_all | solution.py:319
  50.2 12.1 %mix.1 = bf16[64,2,32,64]{3,2,1,0:T(8,128)(2,1)} custom-call(f32[16,2,32,64]{3,2,1,0:T(8,128)S(1)} %maximum_convert_fusion.coeff_ref, bf16[2,16,64,32,64]{4,3,2,1,0:T(8,128)(2,1)} %bitcast.114), custom_call_target="tpu_custom_call" | custom-call | flops 16777216 | bytes 16777216 | tf_op jit(solution)/shard_map/mix/pallas_call | solution.py:96
  62.7 26.8 %reduce-scatter.2.cloned.1.call-done = bf16[16,2,32,64]{3,2,1,0:T(8,128)(2,1)} async-done(((bf16[64,2,32,64]{3,2,1,0:T(8,128)(2,1)}), bf16[16,2,32,64]{3,2,1,0:T(8,128)(2,1)}) %reduce-scatter.2.cloned.1.call-update) | async-done | bytes 131088 | tf_op jit(solution)/shard_map/reduce_scatter | solution.py:325
  103.1 5.2 %all-to-all-start.1 = ((bf16[32,16,8,128]{3,2,1,0:T(8,128)(2,1)}), bf16[32,16,8,128]{3,2,1,0:T(8,128)(2,1)S(1)}, u32[]{:S(2)}, u32[]{:S(2)}) async-start(bf16[32,16,8,128]{3,2,1,0:T(8,128)(2,1)} %copy.38), calls=%async_computation.2 | async-start | bytes 2097152 | tf_op jit(solution)/shard_map/all_to_all | solution.py:331
  108.3 6.4 %broadcast_multiply_fusion = (bf16[64,8,64,8]{3,2,1,0:T(8,128)(2,1)}, bf16[64,8,64,8]{3,2,1,0:T(8,128)(2,1)}) fusion(bf16[64,64]{1,0:T(8,128)(2,1)S(1)} %copy-done.3, bf16[8,8]{1,0:T(8,128)(2,1)S(1)} %fusion.21, bf16[64,64]{1,0:T(8,128)(2,1)S(1)} %copy.40), kind=kLoop, calls=%fused_computation.9 | loop fusion | flops 524288 | bytes 1065088 | tf_op jit(solution)/shard_map/jit(kron)/mul | solution.py:352
  114.7 12.9 %mul.103.back_ref = bf16[512,512]{1,0:T(8,128)(2,1)S(1)} reshape(bf16[64,8,64,8]{3,2,1,0:T(8,128)(2,1)} %get-tuple-element.20) | data formatting | bytes 1048576 | tf_op jit(solution)/shard_map/jit(kron)/mul | solution.py:352
  127.6 12.9 %mul.100.mix_ref = bf16[512,512]{1,0:T(8,128)(2,1)S(1)} reshape(bf16[64,8,64,8]{3,2,1,0:T(8,128)(2,1)} %get-tuple-element.21) | data formatting | bytes 1048576 | tf_op jit(solution)/shard_map/jit(kron)/mul | solution.py:351
  140.5 4.7 %dynamic-slice_bitcast_fusion.1.field_ref = bf16[512,4096]{1,0:T(8,128)(2,1)} fusion(bf16[64,32,4096]{2,1,0:T(8,128)(2,1)} %param.8, s32[]{:T(128)S(6)} %select_n.33), kind=kLoop, calls=%fused_computation.12 | loop fusion | bytes 8388612 | tf_op jit(solution)/shard_map/reshape | solution.py:349
  145.2 4.7 %dynamic-slice_bitcast_fusion.cotangent_ref = bf16[512,4096]{1,0:T(8,128)(2,1)} fusion(bf16[64,32,4096]{2,1,0:T(8,128)(2,1)} %param.9, s32[]{:T(128)S(6)} %select_n.33), kind=kLoop, calls=%fused_computation.11 | loop fusion | bytes 8388612 | tf_op jit(solution)/shard_map/reshape | solution.py:350
  151.1 23.5 %grid.1 = (bf16[512,4096]{1,0:T(8,128)(2,1)}, bf16[512,1024]{1,0:T(8,128)(2,1)S(1)}, f32[512,512]{1,0:T(8,128)S(1)}, f32[512,1]{1,0:T(8,128)S(1)}) custom-call(bf16[512,1024]{1,0:T(8,128)(2,1)} %bitcast.127, bf16[4096,1024]{1,0:T(8,128)(2,1)} %constant.53.clone.table_ref, bf16[512,4096]{1,0:T(8,128)(2,1)} %dynamic-slice_bitcast_fusion.1.field_ref, ...), custom_call_target="tpu_custom_call" | custom-call | flops 15032385536 | bytes 20971520 | tf_op jit(solution)/shard_map/grid/pallas_call | solution.py:236
  176.0 29.4 %all_to_all.26 = bf16[32,16,8,128]{3,2,1,0:T(8,128)(2,1)S(1)} all-to-all(bf16[32,16,8,128]{3,2,1,0:T(8,128)(2,1)S(1)} %bitcast.126), channel_id=1, replica_groups=mesh['slab'=8,'chan'=4] {'slab','chan'}, dimensions={0} | all-to-all | bytes 2097152 | tf_op jit(solution)/shard_map/all_to_all | solution.py:362
  205.4 6.4 %all-to-all-start.4 = ((bf16[4,16,8,4096]{3,2,1,0:T(8,128)(2,1)}), bf16[4,16,8,4096]{3,2,1,0:T(8,128)(2,1)}, u32[]{:S(2)}, u32[]{:S(2)}) async-start(bf16[4,16,8,4096]{3,2,1,0:T(8,128)(2,1)} %bitcast.121), calls=%async_computation.5 | async-start | bytes 8388608 | tf_op jit(solution)/shard_map/all_to_all | solution.py:355
  213.9 4.5 %copy.44 = bf16[16,256,2,64]{1,3,2,0:T(8,128)(2,1)S(1)} copy(bf16[16,256,2,64]{3,2,1,0:T(2,128)(2,1)} %reshape_reshape.4) | data formatting | bytes 2097152 | tf_op jit(solution)/shard_map/reshape;reshape | solution.py:367
  219.8 46.6 %all_gather.3 = bf16[64,2,32,64]{3,2,1,0:T(8,128)(2,1)S(1)} all-gather(bf16[16,2,32,64]{3,2,1,0:T(8,128)(2,1)S(1)} %fusion.18), channel_id=1, replica_groups=mesh['slab'=8,'chan'=4] {'chan'}, dimensions={0}, use_global_device_ids=true | all-gather | bytes 655360 | tf_op jit(solution)/shard_map/all_gather | solution.py:369
  266.7 11.1 %adjoint.1 = bf16[16,2,32,64]{3,2,1,0:T(8,128)(2,1)S(1)} custom-call(f32[64,2,32,64]{3,2,1,0:T(8,128)S(1)} %convert_element_type.56.hat_ref, bf16[2,16,64,32,64]{4,3,2,1,0:T(8,128)(2,1)} %bitcast.115), custom_call_target="tpu_custom_call" | custom-call | flops 16777216 | bytes 16777216 | tf_op jit(solution)/shard_map/adjoint/pallas_call | solution.py:138
  280.3 6.0 %copy.46 = bf16[16,256,2,64]{3,2,1,0:T(2,128)(2,1)} copy(bf16[16,256,2,64]{1,3,2,0:T(8,128)(2,1)} %pad_maximum_fusion.1) | data formatting | bytes 2097152 | tf_op jit(solution)/shard_map/stack | solution.py:292
  286.2 4.7 %convert_element_type.57 = bf16[16,8,32,128]{3,2,1,0:T(8,128)(2,1)} reshape(bf16[16,256,2,64]{3,2,1,0:T(2,128)(2,1)} %copy.46) | data formatting | bytes 2097152 | tf_op jit(solution)/shard_map/convert_element_type | solution.py:373
  293.3 5.3 %all-to-all-start.3 = ((bf16[8,16,32,128]{3,2,1,0:T(8,128)(2,1)}), bf16[8,16,32,128]{3,2,1,0:T(8,128)(2,1)}, u32[]{:S(2)}, u32[]{:S(2)}) async-start(bf16[8,16,32,128]{3,2,1,0:T(8,128)(2,1)} %copy.47), calls=%async_computation.4 | async-start | bytes 2097152 | tf_op jit(solution)/shard_map/all_to_all | solution.py:375
  298.9 11.9 %reshape.119 = f32[64,8,64,8]{3,2,1,0:T(8,128)} reshape(f32[512,512]{1,0:T(8,128)} %copy-done) | data formatting | bytes 2097152 | tf_op jit(solution)/shard_map/reshape | solution.py:385
  310.9 7.5 %select_reduce_fusion = f32[64,64]{1,0:T(8,128)S(1)} fusion(f32[64,8,64,8]{3,2,1,0:T(8,128)} %reshape.119, pred[8,8]{1,0:T(8,128)(4,1)S(1)} %iota_compare_fusion), kind=kLoop, calls=%fused_computation | loop fusion | flops 520192 | bytes 1065024 | tf_op jit(solution)/shard_map/ipop->io/reduce_sum | solution.py:386
  318.4 39.5 %psum.7 = f32[65,64]{1,0:T(8,128)S(1)} all-reduce(f32[65,64]{1,0:T(8,128)S(1)} %maximum_multiply_fusion.1), channel_id=1, replica_groups=mesh['slab'=8,'chan'=4] {'slab','chan'}, use_global_device_ids=true, to_apply=%region_3.4 | all-reduce | flops 4160 | bytes 33280 | tf_op jit(solution)/shard_map/psum | solution.py:389
  359.0 11.7 %outer.1 = f32[2,16,64,32,64]{4,3,2,1,0:T(8,128)} custom-call(f32[16,2,32,64]{3,2,1,0:T(8,128)S(1)} %maximum_convert_fusion.coeff_ref, f32[64,2,32,64]{3,2,1,0:T(8,128)S(1)} %convert_element_type.56.hat_ref), custom_call_target="tpu_custom_call" | custom-call | flops 12582912 | bytes 33554432 | tf_op jit(solution)/shard_map/outer/pallas_call | solution.py:173
  370.7 11.4 %fusion.3 = bf16[16,32,4096]{2,1,0:T(8,128)(2,1)} fusion(bf16[4096,1024]{1,0:T(8,128)(2,1)} %constant.53.clone.table_ref, bf16[4,16,8,4096]{3,2,1,0:T(8,128)(2,1)} %all-to-all-done.4, bf16[8,16,32,128]{3,2,1,0:T(8,128)(2,1)} %all-to-all-done.3), kind=kOutput, calls=%fused_computation.5 | convolution fusion | flops 4301258752 | bytes 17825792 | tf_op jit(solution)/shard_map/dot_general | solution.py:379
  (60 shorter events, 36.8 us)
Async XLA Ops:
  7.2 82.3 %reduce-scatter.2.cloned.1.call-start = ((), (), s32[]{:S(2)}) async-start(), calls=%async_computation.6 | async-start | bytes 1310720 | tf_op jit(solution)/shard_map/reduce_scatter | solution.py:325
  7.2 4.6 %copy-start.5 = (bf16[4096,1024]{1,0:T(8,128)(2,1)S(1)}, bf16[4096,1024]{1,0:T(8,128)(2,1)}, u32[]{:S(2)}) copy-start(bf16[4096,1024]{1,0:T(8,128)(2,1)} %constant.53.clone.table_ref) | copy-start | bytes 25165828
  44.6 4.4 %copy-start.1 = (bf16[32,256,1,1]{1,0,3,2:T(8,128)(2,1)S(1)}, bf16[32,256,1,1]{1,0,3,2:T(8,128)(2,1)}, u32[]{:S(2)}) copy-start(bf16[32,256,1,1]{1,0,3,2:T(8,128)(2,1)} %constant.56) | copy-start | bytes 49156
  48.5 1.0 copy-start.2
  50.2 12.2 %copy-start.3 = (bf16[64,64]{1,0:T(8,128)(2,1)S(1)}, bf16[64,64]{1,0:T(8,128)(2,1)}, u32[]{:S(2)}) copy-start(bf16[64,64]{1,0:T(8,128)(2,1)} %param.11) | copy-start | bytes 24580
  50.2 12.3 %copy-start.4 = (bf16[64]{0:T(256)(128)(2,1)S(1)}, bf16[64]{0:T(256)(128)(2,1)}, u32[]{:S(2)}) copy-start(bf16[64]{0:T(256)(128)(2,1)} %param.12) | copy-start | bytes 388
  103.1 46.7 %all-to-all-start.1 = ((bf16[32,16,8,128]{3,2,1,0:T(8,128)(2,1)}), bf16[32,16,8,128]{3,2,1,0:T(8,128)(2,1)S(1)}, u32[]{:S(2)}, u32[]{:S(2)}) async-start(bf16[32,16,8,128]{3,2,1,0:T(8,128)(2,1)} %copy.38), calls=%async_computation.2 | async-start | bytes 2097152 | tf_op jit(solution)/shard_map/all_to_all | solution.py:331
  174.7 1.1 copy-start
  205.4 87.9 %all-to-all-start.4 = ((bf16[4,16,8,4096]{3,2,1,0:T(8,128)(2,1)}), bf16[4,16,8,4096]{3,2,1,0:T(8,128)(2,1)}, u32[]{:S(2)}, u32[]{:S(2)}) async-start(bf16[4,16,8,4096]{3,2,1,0:T(8,128)(2,1)} %bitcast.121), calls=%async_computation.5 | async-start | bytes 8388608 | tf_op jit(solution)/shard_map/all_to_all | solution.py:355
  293.3 77.4 %all-to-all-start.3 = ((bf16[8,16,32,128]{3,2,1,0:T(8,128)(2,1)}), bf16[8,16,32,128]{3,2,1,0:T(8,128)(2,1)}, u32[]{:S(2)}, u32[]{:S(2)}) async-start(bf16[8,16,32,128]{3,2,1,0:T(8,128)(2,1)} %copy.47), calls=%async_computation.4 | async-start | bytes 2097152 | tf_op jit(solution)/shard_map/all_to_all | solution.py:375
Sparse Core Ops, SparseCore 0:
  62.4 27.0 reduce-scatter.1

commit v2 on v1

v2 whole, which is shorter than its diff:
```python
import functools
import math

import jax
import jax.numpy as jnp
import ml_dtypes
import numpy as np
from jax import lax
from jax.experimental import pallas as pl
from jax.experimental.pallas import tpu as pltpu
from jax.sharding import PartitionSpec as P

MX = 32
MY = 32
MZ = 16
NY = 64
NZ = 64

BF16 = ml_dtypes.bfloat16
VMEM_LIMIT = 50 * 1024 * 1024


def kept_modes(total, length):
    mode_index = np.arange(total, dtype=np.int32)
    return np.where(mode_index < total // 2, mode_index, mode_index - total + length)


def rounded_waves(frequency, length):
    positions = np.arange(length, dtype=np.int32)
    wound_up = frequency[:, None] * positions[None, :] % length
    angle = np.float32(2.0 * math.pi / length) * wound_up.astype(np.float32)
    cosine = np.cos(angle).astype(BF16).astype(np.float32)
    sine = np.sin(angle).astype(BF16).astype(np.float32)
    return cosine, sine


def plane_table(slabs):
    cosine_z, sine_z = rounded_waves(np.arange(MZ, dtype=np.int32), NZ)
    cosine_y, sine_y = rounded_waves(kept_modes(MY, NY), NY)
    cz, sz = cosine_z.T[None, :, :, None], sine_z.T[None, :, :, None]
    cy, sy = cosine_y.T[:, None, None, :], sine_y.T[:, None, None, :]
    real = (cz * cy - sz * sy).reshape(NY * NZ, slabs, 1, -1)
    imag = -(cz * sy + sz * cy).reshape(NY * NZ, slabs, 1, -1)
    return np.concatenate([real, imag], 2).reshape(NY * NZ, -1).astype(BF16)


def line_tables(length):
    cosine, sine = rounded_waves(kept_modes(MX, length), length)
    return cosine.astype(BF16), sine.astype(BF16)


def gelu_grad(pre_act):
    normal_cdf = 0.5 * (1.0 + lax.erf(pre_act * (1.0 / math.sqrt(2.0))))
    normal_pdf = jnp.exp(-0.5 * pre_act * pre_act) * (1.0 / math.sqrt(2.0 * math.pi))
    return normal_cdf + pre_act * normal_pdf


def params():
    return pltpu.CompilerParams(vmem_limit_bytes=VMEM_LIMIT)


def pick(total, wanted):
    return math.gcd(total, wanted)


def turned(modes):
    matrix = np.zeros((2 * modes, 2 * modes), np.float32)
    index = np.arange(modes)
    matrix[modes + index, index] = 1.0
    matrix[index, modes + index] = -1.0
    return matrix.astype(BF16)


def part_of(modes):
    matrix = np.zeros((2, 2 * modes, modes), np.float32)
    index = np.arange(modes)
    matrix[0, index, index] = 1.0
    matrix[1, modes + index, index] = 1.0
    return matrix.astype(BF16)


def wide(a, b):
    return jnp.dot(a, b, preferred_element_type=jnp.float32)


def line_modes(pencil, lines, turn):
    twisted = wide(pencil, turn).astype(jnp.bfloat16)
    return wide(lines, jnp.concatenate([pencil, twisted], 0))


def line_values(spectrum, lines_back, turn_back):
    twisted = wide(spectrum, turn_back).astype(jnp.bfloat16)
    return wide(lines_back, jnp.concatenate([spectrum, twisted], 0))


def whole(shape):
    return pl.BlockSpec(shape, lambda *_: (0,) * len(shape))


def mix_kernel(pencil_ref, lines_ref, turn_ref, part_ref, pack_ref, weight_ref, out_ref, coeff_ref, *, inner):
    group, outs = weight_ref.shape[1], weight_ref.shape[2]
    shape = weight_ref.shape[3:]

    @pl.when(pl.program_id(0) == 0)
    def _():
        def one_channel(i, carry):
            packed = line_modes(pencil_ref[i], lines_ref[...], turn_ref[...]).astype(jnp.bfloat16)
            coeff_ref[i, 0] = wide(packed, part_ref[0])
            coeff_ref[i, 1] = wide(packed, part_ref[1])
            return carry

        lax.fori_loop(0, group, one_channel, 0, unroll=4)

    def some_outputs(step, carry):
        first = step * inner

        def one_input(i, sums):
            real, imag = coeff_ref[i, 0], coeff_ref[i, 1]
            done = []
            for k in range(inner):
                wr = weight_ref[0, i, first + k].astype(jnp.float32)
                wi = weight_ref[1, i, first + k].astype(jnp.float32)
                done.append(sums[2 * k] + (real * wr - imag * wi))
                done.append(sums[2 * k + 1] + (real * wi + imag * wr))
            return tuple(done)

        zero = jnp.zeros(shape, jnp.float32)
        sums = lax.fori_loop(0, group, one_input, (zero,) * (2 * inner), unroll=4)
        for k in range(inner):
            out_ref[first + k] = (
                wide(sums[2 * k].astype(jnp.bfloat16), pack_ref[0])
                + wide(sums[2 * k + 1].astype(jnp.bfloat16), pack_ref[1])
            ).astype(out_ref.dtype)
        return carry

    lax.fori_loop(0, outs // inner, some_outputs, 0)


def mix(pencils, lines, turn, part, pack, weight):
    group, channels, kept, modes = weight.shape[1:]
    block = pick(channels, 8)
    return pl.pallas_call(
        functools.partial(mix_kernel, inner=pick(block, 4)),
        grid=(channels // block,),
        in_specs=[
            whole(pencils.shape), whole(lines.shape), whole(turn.shape), whole(part.shape),
            whole(pack.shape),
            pl.BlockSpec((2, group, block, kept, modes), lambda s: (0, 0, s, 0, 0)),
        ],
        out_specs=[
            pl.BlockSpec((block, kept, 2 * modes), lambda s: (s, 0, 0)),
            whole((group, 2, kept, modes)),
        ],
        out_shape=[
            jax.ShapeDtypeStruct((channels, kept, 2 * modes), jnp.bfloat16),
            jax.ShapeDtypeStruct((group, 2, kept, modes), jnp.float32),
        ],
        compiler_params=params(),
        cost_estimate=pl.CostEstimate(
            flops=4 * weight.size, bytes_accessed=4 * weight.size, transcendentals=0
        ),
        name="mix",
    )(pencils, lines, turn, part, pack, weight)


def spread_kernel(parts_ref, scale_ref, lines_ref, turn_ref, out_ref):
    def one_channel(i, carry):
        total = parts_ref[0, i].astype(jnp.float32)
        for g in range(1, parts_ref.shape[0]):
            total += parts_ref[g, i].astype(jnp.float32)
        spectrum = (total * scale_ref[...]).astype(jnp.bfloat16)
        out_ref[i] = line_values(spectrum, lines_ref[...], turn_ref[...]).astype(out_ref.dtype)
        return carry

    lax.fori_loop(0, parts_ref.shape[1], one_channel, 0, unroll=4)


def spread(parts, scale, lines, turn):
    group, width = parts.shape[1], parts.shape[3]
    shape = (group, lines.shape[0], width)
    return pl.pallas_call(
        spread_kernel,
        out_shape=jax.ShapeDtypeStruct(shape, jnp.bfloat16),
        compiler_params=params(),
        name="spread",
    )(parts, scale, lines, turn)


def gather_lines_kernel(pencil_ref, scale_ref, lines_ref, turn_ref, out_ref):
    def one_channel(i, carry):
        packed = line_modes(pencil_ref[i], lines_ref[...], turn_ref[...])
        out_ref[i] = (packed * scale_ref[...]).astype(out_ref.dtype)
        return carry

    lax.fori_loop(0, pencil_ref.shape[0], one_channel, 0, unroll=4)


def gather_lines(pencils, scale, lines, turn):
    shape = (pencils.shape[0], lines.shape[0], pencils.shape[2])
    return pl.pallas_call(
        gather_lines_kernel,
        out_shape=jax.ShapeDtypeStruct(shape, jnp.bfloat16),
        compiler_params=params(),
        name="lines",
    )(pencils, scale, lines, turn)


def adjoint_kernel(hat_ref, lines_ref, turn_ref, part_ref, pack_ref, weight_ref, out_ref, wide_ref):
    own, channels = weight_ref.shape[1], weight_ref.shape[2]
    shape = weight_ref.shape[3:]

    @pl.when(pl.program_id(0) == 0)
    def _():
        def one_channel(o, carry):
            wide_ref[o, 0] = wide(hat_ref[o], part_ref[0])
            wide_ref[o, 1] = wide(hat_ref[o], part_ref[1])
            return carry

        lax.fori_loop(0, channels, one_channel, 0, unroll=4)

    def one_output(o, sums):
        real, imag = wide_ref[o, 0], wide_ref[o, 1]
        done = []
        for k in range(own):
            wr = weight_ref[0, k, o].astype(jnp.float32)
            wi = weight_ref[1, k, o].astype(jnp.float32)
            done.append(sums[2 * k] + (real * wr + imag * wi))
            done.append(sums[2 * k + 1] + (imag * wr - real * wi))
        return tuple(done)

    zero = jnp.zeros(shape, jnp.float32)
    sums = lax.fori_loop(0, channels, one_output, (zero,) * (2 * own), unroll=4)
    for k in range(own):
        packed = wide(sums[2 * k].astype(jnp.bfloat16), pack_ref[0]) + wide(
            sums[2 * k + 1].astype(jnp.bfloat16), pack_ref[1]
        )
        values = line_values(packed.astype(jnp.bfloat16), lines_ref[...], turn_ref[...])
        out_ref[k] = values.astype(out_ref.dtype)


def adjoint_of(hat, lines, turn, part, pack, weight):
    group, channels, kept, modes = weight.shape[1:]
    block = pick(group, 2)
    length = lines.shape[0]
    return pl.pallas_call(
        adjoint_kernel,
        grid=(group // block,),
        in_specs=[
            whole(hat.shape), whole(lines.shape), whole(turn.shape), whole(part.shape),
            whole(pack.shape),
            pl.BlockSpec((2, block, channels, kept, modes), lambda s: (0, s, 0, 0, 0)),
        ],
        out_specs=[
            pl.BlockSpec((block, length, 2 * modes), lambda s: (s, 0, 0)),
            whole((channels, 2, kept, modes)),
        ],
        out_shape=[
            jax.ShapeDtypeStruct((group, length, 2 * modes), jnp.bfloat16),
            jax.ShapeDtypeStruct((channels, 2, kept, modes), jnp.float32),
        ],
        compiler_params=params(),
        cost_estimate=pl.CostEstimate(
            flops=4 * weight.size, bytes_accessed=4 * weight.size, transcendentals=0
        ),
        name="adjoint",
    )(hat, lines, turn, part, pack, weight)


def outer_kernel(coeff_ref, hat_ref, out_ref):
    own, channels = out_ref.shape[1], out_ref.shape[2]
    for i in range(own):
        cr, ci = coeff_ref[i, 0], coeff_ref[i, 1]

        def one_output(o, carry):
            hr, hi = hat_ref[o, 0], hat_ref[o, 1]
            out_ref[0, i, o] = cr * hr + ci * hi
            out_ref[1, i, o] = cr * hi - ci * hr
            return carry

        lax.fori_loop(0, channels, one_output, 0, unroll=4)


def outer(coeff, hat):
    group, _, lines, modes = coeff.shape
    channels = hat.shape[0]
    block = pick(group, 2)
    return pl.pallas_call(
        outer_kernel,
        grid=(group // block,),
        in_specs=[
            pl.BlockSpec((block, 2, lines, modes), lambda s: (s, 0, 0, 0)),
            pl.BlockSpec((channels, 2, lines, modes), lambda s: (0, 0, 0, 0)),
        ],
        out_specs=pl.BlockSpec((2, block, channels, lines, modes), lambda s: (0, s, 0, 0, 0)),
        out_shape=jax.ShapeDtypeStruct((2, group, channels, lines, modes), jnp.float32),
        compiler_params=params(),
        cost_estimate=pl.CostEstimate(
            flops=6 * group * channels * lines * modes,
            bytes_accessed=16 * group * channels * lines * modes,
            transcendentals=0,
        ),
        name="outer",
    )(coeff, hat)


ROWS_BY_ROWS = (((1,), (1,)), ((), ()))


def grid_kernel(
    modes_ref, table_ref, field_ref, cotangent_ref, point_weight_ref, repeat_ref, bias_ref,
    point_ref, hat_ref, sums_ref, total, weight_total, bias_total, mix_ref, back_ref, *, planes,
):
    step = pl.program_id(0)
    rows, channels = repeat_ref.shape

    def same_plane():
        first = lax.broadcasted_iota(jnp.int32, (rows, rows), 0) % planes
        return first == lax.broadcasted_iota(jnp.int32, (rows, rows), 1) % planes

    @pl.when(step == 0)
    def _():
        total[...] = jnp.zeros_like(total)
        weight_total[...] = jnp.zeros_like(weight_total)
        bias_total[...] = jnp.zeros_like(bias_total)
        repeat = repeat_ref[...]
        half = wide(repeat, point_weight_ref[...]).astype(jnp.bfloat16)
        full = lax.dot_general(half, repeat, ROWS_BY_ROWS, preferred_element_type=jnp.float32)
        back = jnp.where(same_plane(), full, 0.0)
        back_ref[...] = back.astype(jnp.bfloat16)
        mix_ref[...] = back.T.astype(jnp.bfloat16)

    table = table_ref[...]
    field = field_ref[...]
    pre_act = lax.dot_general(
        modes_ref[...], table, ROWS_BY_ROWS, preferred_element_type=jnp.float32
    )
    pre_act += jnp.dot(mix_ref[...], field, preferred_element_type=jnp.float32)
    pre_act += bias_ref[...]
    grad_wide = cotangent_ref[...].astype(jnp.float32) * gelu_grad(pre_act)
    grad_pre = grad_wide.astype(jnp.bfloat16)
    point_ref[...] = jnp.dot(
        back_ref[...], grad_pre, preferred_element_type=jnp.float32
    ).astype(point_ref.dtype)
    total[...] += jnp.dot(grad_pre, table, preferred_element_type=jnp.float32)
    weight_total[...] += lax.dot_general(
        field, grad_pre, ROWS_BY_ROWS, preferred_element_type=jnp.float32
    )
    bias_total[...] += jnp.sum(grad_pre.astype(jnp.float32), axis=1, keepdims=True)

    @pl.when(step == pl.num_programs(0) - 1)
    def _():
        width = hat_ref.shape[-1]
        for s in range(hat_ref.shape[0]):
            hat_ref[s] = total[:, s * width : (s + 1) * width].astype(hat_ref.dtype)
        repeat = repeat_ref[...].astype(jnp.float32)
        kept = jnp.where(same_plane(), weight_total[...], 0.0)
        columns = jnp.dot(
            kept, repeat, precision=lax.Precision.HIGHEST, preferred_element_type=jnp.float32
        )
        both = (((0,), (0,)), ((), ()))
        sums_ref[:channels] = lax.dot_general(
            repeat, columns, both, precision=lax.Precision.HIGHEST,
            preferred_element_type=jnp.float32,
        )
        spread_bias = jnp.broadcast_to(bias_total[...], (rows, 8))
        sums_ref[channels:] = lax.dot_general(
            spread_bias, repeat, both, precision=lax.Precision.HIGHEST,
            preferred_element_type=jnp.float32,
        )


def grid_stage(modes, table, field, cotangent, point_weight, bias, planes, parts):
    rows, width = modes.shape
    cells = table.shape[0]
    channels = point_weight.shape[0]
    block = pick(cells, 512)
    along = lambda s: (0, s)
    repeat = jnp.asarray(np.repeat(np.eye(channels, dtype=np.float32), planes, 0).astype(BF16))
    return pl.pallas_call(
        functools.partial(grid_kernel, planes=planes),
        grid=(cells // block,),
        in_specs=[
            whole((rows, width)),
            pl.BlockSpec((block, width), lambda s: (s, 0)),
            pl.BlockSpec((rows, block), along),
            pl.BlockSpec((rows, block), along),
            whole((channels, channels)),
            whole((rows, channels)),
            whole((rows, 1)),
        ],
        out_specs=[
            pl.BlockSpec((rows, block), along),
            whole((parts, rows, width // parts)),
            whole((channels + 8, channels)),
        ],
        out_shape=[
            jax.ShapeDtypeStruct((rows, cells), jnp.bfloat16),
            jax.ShapeDtypeStruct((parts, rows, width // parts), jnp.bfloat16),
            jax.ShapeDtypeStruct((channels + 8, channels), jnp.float32),
        ],
        scratch_shapes=[
            pltpu.VMEM((rows, width), jnp.float32),
            pltpu.VMEM((rows, rows), jnp.float32),
            pltpu.VMEM((rows, 1), jnp.float32),
            pltpu.VMEM((rows, rows), jnp.bfloat16),
            pltpu.VMEM((rows, rows), jnp.bfloat16),
        ],
        compiler_params=params(),
        cost_estimate=pl.CostEstimate(
            flops=2 * rows * cells * (2 * width + 3 * rows),
            bytes_accessed=2 * cells * (width + 3 * rows),
            transcendentals=2 * rows * cells,
        ),
        name="grid",
    )(modes, table, field, cotangent, point_weight, repeat, bias)


def finish_kernel(modes_ref, table_ref, point_ref, out_ref):
    back = lax.dot_general(
        modes_ref[...], table_ref[...], ROWS_BY_ROWS, preferred_element_type=jnp.float32
    )
    point = jnp.swapaxes(point_ref[...].astype(jnp.float32), 0, 1)
    out_ref[...] = (back + point.reshape(back.shape)).astype(out_ref.dtype)


def finish(modes, table, point):
    chans, group, planes, cells = point.shape
    rows, width = modes.shape
    block = pick(cells, 512)
    return pl.pallas_call(
        finish_kernel,
        grid=(cells // block,),
        in_specs=[
            whole((rows, width)),
            pl.BlockSpec((block, width), lambda s: (s, 0)),
            pl.BlockSpec((chans, group, planes, block), lambda s: (0, 0, 0, s)),
        ],
        out_specs=pl.BlockSpec((rows, block), lambda s: (0, s)),
        out_shape=jax.ShapeDtypeStruct((rows, cells), jnp.bfloat16),
        compiler_params=params(),
        cost_estimate=pl.CostEstimate(
            flops=2 * rows * cells * width,
            bytes_accessed=2 * cells * (width + 2 * rows),
            transcendentals=0,
        ),
        name="finish",
    )(modes, table, point)


def begin_kernel(chan_ref, field_ref, table_ref, out_ref, total):
    step = pl.program_id(0)
    field = field_ref[...].reshape(total.shape[0], field_ref.shape[2])
    part = wide(field, table_ref[...])

    @pl.when(step == 0)
    def _():
        total[...] = part

    @pl.when(step > 0)
    def _():
        total[...] += part

    @pl.when(step == pl.num_programs(0) - 1)
    def _():
        width = out_ref.shape[-1]
        for s in range(out_ref.shape[0]):
            out_ref[s] = total[:, s * width : (s + 1) * width].astype(out_ref.dtype)


def begin(chan_index, field, table, group, parts):
    planes, cells = field.shape[1:]
    width = table.shape[1]
    rows = group * planes
    block = pick(cells, 1024)
    return pl.pallas_call(
        begin_kernel,
        grid_spec=pltpu.PrefetchScalarGridSpec(
            num_scalar_prefetch=1,
            grid=(cells // block,),
            in_specs=[
                pl.BlockSpec((group, planes, block), lambda s, chan: (chan[0], 0, s)),
                pl.BlockSpec((block, width), lambda s, chan: (s, 0)),
            ],
            out_specs=whole((parts, rows, width // parts)),
            scratch_shapes=[pltpu.VMEM((rows, width), jnp.float32)],
        ),
        out_shape=jax.ShapeDtypeStruct((parts, rows, width // parts), jnp.bfloat16),
        compiler_params=params(),
        cost_estimate=pl.CostEstimate(
            flops=2 * rows * cells * width,
            bytes_accessed=2 * cells * (width + rows),
            transcendentals=0,
        ),
        name="begin",
    )(chan_index.reshape(1), field, table)


def exchange_kernel(axes, sizes, blocks, *refs):
    count = len(blocks)
    ins, outs = refs[:count], refs[count : 2 * count]
    send, recv, local = refs[2 * count :]
    total = math.prod(sizes)
    last = sizes[-1]
    me = lax.axis_index(axes[0])
    if len(axes) == 2:
        me = me * last + lax.axis_index(axes[1])

    def place(index):
        if len(axes) == 2:
            return {axes[0]: lax.div(index, last), axes[1]: lax.rem(index, last)}
        return {axes[0]: index}

    def source(a, index):
        if blocks[a] == total:
            return ins[a].at[index]
        if blocks[a] == 1:
            return ins[a].at[0]
        return ins[a].at[lax.rem(index, last)]

    def copy(a, shift):
        peer = lax.rem(me + shift, total)
        return pltpu.make_async_remote_copy(
            src_ref=source(a, peer),
            dst_ref=outs[a].at[me],
            send_sem=send.at[a, shift],
            recv_sem=recv.at[a, shift],
            device_id=place(peer),
            device_id_type=pl.DeviceIdType.MESH,
        )

    barrier = pltpu.get_barrier_semaphore()

    def greet(shift, carry):
        pl.semaphore_signal(
            barrier, inc=1, device_id=place(lax.rem(me + shift, total)),
            device_id_type=pl.DeviceIdType.MESH,
        )
        return carry

    def start(shift, carry):
        for a in range(count):
            copy(a, shift).start()
        return carry

    def wait(shift, carry):
        for a in range(count):
            copy(a, shift).wait()
        return carry

    lax.fori_loop(1, total, greet, 0)
    own = [
        pltpu.make_async_copy(source(a, me), outs[a].at[me], local.at[a]) for a in range(count)
    ]
    for one in own:
        one.start()
    pl.semaphore_wait(barrier, total - 1)
    lax.fori_loop(1, total, start, 0)
    for one in own:
        one.wait()
    lax.fori_loop(1, total, wait, 0)


def exchange(arrays, axes, sizes, collective_id):
    total = math.prod(sizes)
    blocks = tuple(array.shape[0] for array in arrays)
    anywhere = pl.BlockSpec(memory_space=pl.ANY)
    return pl.pallas_call(
        functools.partial(exchange_kernel, axes, sizes, blocks),
        in_specs=[anywhere] * len(arrays),
        out_specs=[anywhere] * len(arrays),
        out_shape=[
            jax.ShapeDtypeStruct((total,) + array.shape[1:], array.dtype) for array in arrays
        ],
        scratch_shapes=[
            pltpu.SemaphoreType.DMA((len(arrays), total)),
            pltpu.SemaphoreType.DMA((len(arrays), total)),
            pltpu.SemaphoreType.DMA((len(arrays),)),
        ],
        compiler_params=pltpu.CompilerParams(
            collective_id=collective_id, has_side_effects=True, vmem_limit_bytes=VMEM_LIMIT
        ),
        cost_estimate=pl.CostEstimate(
            flops=0, bytes_accessed=sum(8 * 2 * a.size for a in arrays), transcendentals=0
        ),
        name="exchange",
    )(*arrays)


def pad_planes(array, dim, spare):
    if not spare:
        return array
    return jnp.pad(array, [(0, spare if d == dim else 0) for d in range(array.ndim)])


def body(slabs, chans, field, cotangent, spectral_weight, point_weight, point_bias):
    channels, planes, cells = field.shape
    group = spectral_weight.shape[1]
    modes = spectral_weight.shape[3]
    own_planes = -(-planes // chans)
    spare = own_planes * chans - planes
    length = planes * slabs
    width = 2 * modes
    tiled = planes % 16 == 0 and own_planes % 8 == 0 and width % 128 == 0
    everyone = ("slab", "chan"), (slabs, chans)
    table = lax.optimization_barrier(jnp.asarray(plane_table(slabs)))
    cosine, sine = line_tables(length)
    lines = jnp.asarray(np.concatenate([cosine, sine], 1))
    lines_back = jnp.asarray(np.concatenate([cosine.T, sine.T], 1))
    turn, turn_back = jnp.asarray(turned(modes)), jnp.asarray(turned(modes).T)
    part, pack = jnp.asarray(part_of(modes)), jnp.asarray(np.swapaxes(part_of(modes), 1, 2))
    slab_index = lax.axis_index("slab")
    chan_index = lax.axis_index("chan")
    weight = jnp.swapaxes(spectral_weight, 3, 4)
    mode_index = slab_index * modes + jnp.arange(width, dtype=jnp.int32) % modes
    scale = (jnp.where(mode_index // MY == 0, 1.0, 2.0) / (length * cells)).astype(jnp.float32)
    scale = scale[None]

    if tiled:
        sections = begin(chan_index, field, table, group, slabs)
    else:
        own_field = lax.dynamic_slice_in_dim(field, chan_index * group, group, 0)
        sections = wide(own_field.reshape(group * planes, cells), table).astype(jnp.bfloat16)
        sections = jnp.moveaxis(sections.reshape(group * planes, slabs, width), 1, 0)
    (pencils,) = exchange([sections], ("slab",), (slabs,), 0)
    pencils = jnp.moveaxis(pencils.reshape(slabs, group, planes, width), 1, 0)
    partial, coeff = mix(
        pencils.reshape(group, length, width), lines, turn, part, pack, weight
    )
    (parts,) = exchange([partial.reshape(chans, group, MX, width)], ("chan",), (chans,), 1)
    pencils = spread(parts, scale, lines_back, turn_back)
    pencils = pad_planes(pencils.reshape(group, slabs, planes, width), 2, spare)
    pencils = pencils.reshape(group, slabs, chans, own_planes, width)
    pencils = jnp.transpose(pencils, (1, 2, 0, 3, 4))
    pencils = pencils.reshape(slabs * chans, group, own_planes, width)
    slabs_in = lax.all_to_all(
        pencils, ("slab", "chan"), split_axis=0, concat_axis=0, tiled=True
    )
    slabs_in = slabs_in.reshape(slabs, channels, own_planes, width)
    rows = channels * own_planes
    slabs_in = jnp.transpose(slabs_in, (1, 2, 0, 3)).reshape(rows, slabs * width)

    first_plane = chan_index * own_planes
    plane_field = lax.dynamic_slice_in_dim(
        pad_planes(field, 1, spare), first_plane, own_planes, 1
    )
    plane_cotangent = lax.dynamic_slice_in_dim(
        pad_planes(cotangent, 1, spare), first_plane, own_planes, 1
    )
    point, hat_rows, sums = grid_stage(
        slabs_in,
        table,
        plane_field.reshape(rows, cells),
        plane_cotangent.reshape(rows, cells),
        point_weight,
        jnp.repeat(point_bias.astype(jnp.float32), own_planes)[:, None],
        own_planes,
        slabs if tiled else 1,
    )
    point = lax.all_to_all(
        point.reshape(chans, group, own_planes, cells),
        "chan", split_axis=0, concat_axis=0, tiled=True,
    )
    if not tiled:
        hat_rows = jnp.moveaxis(hat_rows.reshape(rows, slabs, width), 1, 0)
    hat_rows = hat_rows.reshape(slabs * chans, group, own_planes, width)
    own_sums = sums[:channels].reshape(chans, group, channels)
    bias_sums = jnp.broadcast_to(sums[channels:][None], (chans, 8, channels))
    own_sums = jnp.concatenate([own_sums, bias_sums], 1)
    pencils, all_sums = exchange([hat_rows, own_sums], *everyone, 2)
    pencils = jnp.moveaxis(pencils.reshape(slabs, chans, group, own_planes, width), 2, 0)
    pencils = pencils.reshape(group, slabs, chans * own_planes, width)[:, :, :planes]
    part_hat = gather_lines(pencils.reshape(group, length, width), scale, lines, turn)
    (hat,) = exchange([part_hat[None]], ("chan",), (chans,), 3)

    pencils, hat = adjoint_of(
        hat.reshape(channels, MX, width), lines_back, turn_back, part, pack, weight
    )
    pencils = pencils.reshape(group, slabs, planes, width)
    pencils = lax.all_to_all(
        jnp.moveaxis(pencils, 1, 0), "slab", split_axis=0, concat_axis=0, tiled=True
    )
    grad_spectral = jnp.swapaxes(outer(coeff, hat), 3, 4)
    pencils = jnp.moveaxis(pencils, 0, 2).reshape(group * planes, slabs * width)
    if tiled:
        grad_input = finish(pencils, table, point).reshape(group, planes, cells)
    else:
        back = lax.dot_general(pencils, table, ROWS_BY_ROWS, preferred_element_type=jnp.float32)
        back = back.reshape(group, planes, cells)
        point = jnp.moveaxis(point, 0, 1).reshape(group, chans * own_planes, cells)[:, :planes]
        grad_input = (back + point.astype(jnp.float32)).astype(jnp.bfloat16)

    sums = jnp.sum(all_sums, 0) * (1.0 / math.sqrt(length * cells))
    return (grad_input, grad_spectral, sums[:group], sums[group])


def solution(mesh):
    placed = (
        P(None, "slab", None),
        P(None, "slab", None),
        P(None, "chan", None, "slab", None),
        P(),
        P(),
    )
    return jax.shard_map(
        functools.partial(body, mesh.shape["slab"], mesh.shape["chan"]),
        mesh=mesh,
        in_specs=placed,
        out_specs=(
            P("chan", "slab", None),
            P(None, "chan", None, "slab", None),
            P("chan", None),
            P(),
        ),
        check_vma=False,
    )
```

time: 392 us -> 284 us (0.72)
  Pallas kernels: 58.4 us -> 179 us
  blocking collectives: 144 us -> 27.1 us
  local copies, waits for them, and re-layouts: 89.8 us -> 12.3 us
  waiting for transfers between devices: 26.8 us -> 49.1 us
  matrix products: 21.9 us -> 0 us
  other arithmetic: 17.1 us -> 0.08 us
  between operations: 14.3 us -> 0.93 us
  starting transfers between devices: 17 us -> 11.8 us
    pallas_call x2 -> x10, Pallas kernels: 34.7 us -> 150 us  [the longest x4 85 us: exchange(): pl.pallas_call(functools.partial(exchange_kernel, axes, sizes, blocks), i...]
    all_gather x1 -> x0, blocking collectives: 46.6 us -> none  [body(): lax.all_gather(part_hat, 'chan', axis=0, tiled=True).astype(jnp.float32)]
    psum x1 -> x0, blocking collectives: 39.5 us -> none  [body(): sums = lax.psum(sums, ('slab', 'chan'))]
    all_to_all x1, waiting for transfers between devices: 0.01 us -> 33.6 us  [body(): lax.all_to_all(point.reshape(chans, group, own_planes, cells), 'chan', sp...]
    all_to_all x2 -> x1, blocking collectives: 57.5 us -> 27.1 us  [body(): lax.all_to_all(jnp.moveaxis(pencils, 1, 0), 'slab', split_axis=0, concat_...]
    reduce_scatter x1 -> x0, waiting for transfers between devices: 26.8 us -> none  [body(): spectra = lax.psum_scatter(partial, 'chan', scatter_dimension=0, tiled=True)]
    mul x4 -> x0, local copies, waits for them, and re-layouts: 25.8 us -> none  [the longest x1 12.9 us: body(): jnp.kron(point_weight.T, eye)]
    reshape x7 -> x2, local copies, waits for them, and re-layouts: 22.7 us -> 0.2 us  [the longest x1 0.11 us: body(): pencils = jnp.moveaxis(pencils.reshape(slabs, group, planes, width), 1, 0)]
  transfers between devices with their start and end apart: 4 -> 2, of which waited for: 1 -> 2; matrix products, arithmetic and copies ran while one was open for 22% -> 4% of each run, Pallas kernels for 6% -> 4%
where the time goes in v2:
time: 284 us; the launch traced here: 280 us
  Pallas kernels  179 us (63%)
  waiting for transfers between devices  49.1 us (17%)
  blocking collectives  27.1 us (10%)
  local copies, waits for them, and re-layouts  12.3 us (4%)
  starting transfers between devices  11.8 us (4%)
    pallas_call x4, Pallas kernels, exchange(): pl.pallas_call(functools.partial(exchange_kernel, axes, sizes, blocks), i...  85 us
    all_to_all x1, waiting for transfers between devices, body(): lax.all_to_all(point.reshape(chans, group, own_planes, cells), 'chan', sp...  33.6 us
    all_to_all x1, blocking collectives, body(): lax.all_to_all(jnp.moveaxis(pencils, 1, 0), 'slab', split_axis=0, concat_...  27.1 us
    pallas_call x1, Pallas kernels, grid_stage(): pl.pallas_call(functools.partial(grid_kernel, planes=planes), grid=(cells...  25.1 us
    pallas_call x1, Pallas kernels, mix(): pl.pallas_call(functools.partial(mix_kernel, inner=pick(block, 4)), grid=...  17.2 us
    pallas_call x1, Pallas kernels, adjoint_of(): pl.pallas_call(adjoint_kernel, grid=(group // block,), in_specs=[whole(ha...  16.9 us
    all_to_all x1, waiting for transfers between devices, body(): lax.all_to_all(pencils, ('slab', 'chan'), split_axis=0, concat_axis=0, ti...  15.5 us
    pallas_call x1, Pallas kernels, outer(): pl.pallas_call(outer_kernel, grid=(group // block,), in_specs=[pl.BlockSp...  11.7 us
  transfers between devices with their start and end apart: 2, of which 2 were waited for; matrix products, arithmetic and copies ran while one was open for 4% of the time, Pallas kernels for 4%

profile of v2, /device:TPU:13, one launch (start us, length us, event | category | flops | bytes accessed | tf_op | source)
XLA Modules:
  0.0 280.0 jit_solution(11873623163806233770)
XLA Ops:
  0.7 8.4 %begin.1.refs_0_ = bf16[8,512,128]{2,1,0:T(8,128)(2,1)S(1)} custom-call(s32[1]{0:T(128)} %bitcast.chan_ref, bf16[64,32,4096]{2,1,0:T(8,128)(2,1)} %field_ref.1, bf16[4096,1024]{1,0:T(8,128)(2,1)} %constant.72.clone.table_ref), custom_call_target="tpu_custom_call" | custom-call | flops 4294967296 | bytes 12582912 | tf_op jit(solution)/shard_map/begin/pallas_call | solution.py:475
  9.2 27.3 %exchange.4 = bf16[8,512,128]{2,1,0:T(8,128)(2,1)S(1)} custom-call(bf16[8,512,128]{2,1,0:T(8,128)(2,1)S(1)} %begin.1.refs_0_), custom_call_target="tpu_custom_call" | custom-call | bytes 8388608 | tf_op jit(solution)/shard_map/exchange/pallas_call | solution.py:567
  36.7 17.2 %mix.1 = (bf16[64,32,128]{2,1,0:T(8,128)(2,1)S(1)}, f32[16,2,32,64]{3,2,1,0:T(8,128)S(1)}) custom-call(bf16[16,256,128]{2,1,0:T(8,128)(2,1)S(1)} %bitcast.45, bf16[32,512]{1,0:T(8,128)(2,1)S(1)} %copy-done.5, bf16[128,128]{1,0:T(8,128)(2,1)S(1)} %copy-done.4, bf16[2,128,64]{2,1,0:T(8,128)(2,1)S(1)} %copy-done, bf16[2,64,128]{2,1,0:T(8,128)(2,1)S(1)} %copy-done.2, ...), custom_call_target="tpu_custom_call" | custom-call | flops 16777216 | bytes 16777216 | tf_op jit(solution)/shard_map/mix/pallas_call | solution.py:142
  53.9 8.6 %exchange.5.parts_ref = bf16[4,16,32,128]{3,2,1,0:T(8,128)(2,1)S(1)} custom-call(bf16[4,16,32,128]{3,2,1,0:T(8,128)(2,1)S(1)} %bitcast.55), custom_call_target="tpu_custom_call" | custom-call | bytes 4194304 | tf_op jit(solution)/shard_map/exchange/pallas_call | solution.py:567
  62.5 1.8 spread.1
  64.4 1.3 copy.27
  65.6 5.5 %all-to-all-start = ((bf16[32,16,8,128]{3,2,1,0:T(8,128)(2,1)}), bf16[32,16,8,128]{3,2,1,0:T(8,128)(2,1)S(1)}, u32[]{:S(2)}, u32[]{:S(2)}) async-start(bf16[32,16,8,128]{3,2,1,0:T(8,128)(2,1)} %bitcast.8), calls=%async_computation | async-start | bytes 2097152 | tf_op jit(solution)/shard_map/all_to_all | solution.py:635
  71.3 8.0 %dynamic-slice_bitcast_fusion = (bf16[512,4096]{1,0:T(8,128)(2,1)}, bf16[512,4096]{1,0:T(8,128)(2,1)}) fusion(bf16[64,32,4096]{2,1,0:T(8,128)(2,1)} %param.14, s32[]{:T(128)S(6)} %select_n.44, bf16[64,32,4096]{2,1,0:T(8,128)(2,1)} %field_ref.1), kind=kLoop, calls=%fused_computation | loop fusion | bytes 16777220 | tf_op jit(solution)/shard_map/reshape | solution.py:653
  79.3 15.5 %all-to-all-done = bf16[32,16,8,128]{3,2,1,0:T(8,128)(2,1)S(1)} async-done(((bf16[32,16,8,128]{3,2,1,0:T(8,128)(2,1)}), bf16[32,16,8,128]{3,2,1,0:T(8,128)(2,1)S(1)}, u32[]{:S(2)}, u32[]{:S(2)}) %all-to-all-start) | async-done | bytes 1048608 | tf_op jit(solution)/shard_map/all_to_all | solution.py:635
  94.8 0.3 copy.39
  95.1 25.1 %grid.1 = (bf16[512,4096]{1,0:T(8,128)(2,1)}, bf16[8,512,128]{2,1,0:T(8,128)(2,1)S(1)}, f32[72,64]{1,0:T(8,128)S(1)}) custom-call(bf16[512,1024]{1,0:T(8,128)(2,1)S(1)} %bitcast.51, bf16[4096,1024]{1,0:T(8,128)(2,1)} %constant.72.clone.table_ref, bf16[512,4096]{1,0:T(8,128)(2,1)} %get-tuple-element.23.field_ref, ...), custom_call_target="tpu_custom_call" | custom-call | flops 15032385536 | bytes 20971520 | tf_op jit(solution)/shard_map/grid/pallas_call | solution.py:379
  120.3 39.6 %exchange.6 = (bf16[32,16,8,128]{3,2,1,0:T(8,128)(2,1)S(1)}, f32[32,24,64]{2,1,0:T(8,128)S(1)}) custom-call(bf16[32,16,8,128]{3,2,1,0:T(8,128)(2,1)S(1)} %bitcast.50, f32[4,24,64]{2,1,0:T(8,128)S(1)} %pad_maximum_fusion.refs_1_), custom_call_target="tpu_custom_call" | custom-call | bytes 8486912 | tf_op jit(solution)/shard_map/exchange/pallas_call | solution.py:567
  160.2 1.6 lines.1
  161.8 9.5 %exchange.7 = bf16[4,16,32,128]{3,2,1,0:T(8,128)(2,1)S(1)} custom-call(bf16[1,16,32,128]{3,2,1,0:T(8,128)(2,1)S(1)} %bitcast.54), custom_call_target="tpu_custom_call" | custom-call | bytes 1048576 | tf_op jit(solution)/shard_map/exchange/pallas_call | solution.py:567
  171.3 16.9 %adjoint.1 = (bf16[16,256,128]{2,1,0:T(8,128)(2,1)S(1)}, f32[64,2,32,64]{3,2,1,0:T(8,128)S(1)}) custom-call(bf16[64,32,128]{2,1,0:T(8,128)(2,1)S(1)} %bitcast.49, bf16[256,64]{1,0:T(8,128)(2,1)S(1)} %copy-done.1, bf16[128,128]{1,0:T(8,128)(2,1)S(1)} %copy-done.3, bf16[2,128,64]{2,1,0:T(8,128)(2,1)S(1)} %copy-done, bf16[2,64,128]{2,1,0:T(8,128)(2,1)S(1)} %copy-done.2, ...), custom_call_target="tpu_custom_call" | custom-call | flops 16777216 | bytes 16777216 | tf_op jit(solution)/shard_map/adjoint/pallas_call | solution.py:245
  188.3 27.1 %all_to_all.15 = bf16[8,16,32,128]{3,2,1,0:T(8,128)(2,1)} all-to-all(bf16[8,16,32,128]{3,2,1,0:T(8,128)(2,1)S(1)} %bitcast.63), channel_id=1, replica_groups=mesh['slab'=8,'chan'=4] {'slab'}, dimensions={0} | all-to-all | bytes 2097152 | tf_op jit(solution)/shard_map/all_to_all | solution.py:679
  215.3 6.4 %all-to-all-start.2 = ((bf16[4,16,8,4096]{3,2,1,0:T(8,128)(2,1)}), bf16[4,16,8,4096]{3,2,1,0:T(8,128)(2,1)}, u32[]{:S(2)}, u32[]{:S(2)}) async-start(bf16[4,16,8,4096]{3,2,1,0:T(8,128)(2,1)} %bitcast.60), calls=%async_computation.2 | async-start | bytes 8388608 | tf_op jit(solution)/shard_map/all_to_all | solution.py:659
  221.7 0.6 slice.16
  222.3 11.7 %outer.1 = f32[2,16,64,32,64]{4,3,2,1,0:T(8,128)} custom-call(f32[16,2,32,64]{3,2,1,0:T(8,128)S(1)} %get-tuple-element.19.coeff_ref, f32[64,2,32,64]{3,2,1,0:T(8,128)S(1)} %get-tuple-element.20.hat_ref), custom_call_target="tpu_custom_call" | custom-call | flops 12582912 | bytes 33554432 | tf_op jit(solution)/shard_map/outer/pallas_call | solution.py:287
  234.0 0.5 slice_bitcast_fusion
  234.5 0.7 copy.32
  235.2 0.3 copy.37
  235.5 33.6 %all-to-all-done.2.point_ref = bf16[4,16,8,4096]{3,2,1,0:T(8,128)(2,1)} async-done(((bf16[4,16,8,4096]{3,2,1,0:T(8,128)(2,1)}), bf16[4,16,8,4096]{3,2,1,0:T(8,128)(2,1)}, u32[]{:S(2)}, u32[]{:S(2)}) %all-to-all-start.2) | async-done | bytes 4194336 | tf_op jit(solution)/shard_map/all_to_all | solution.py:659
  269.1 10.9 %finish.1 = bf16[512,4096]{1,0:T(8,128)(2,1)} custom-call(bf16[512,1024]{1,0:T(8,128)(2,1)S(1)} %bitcast.44, bf16[4096,1024]{1,0:T(8,128)(2,1)} %constant.72.clone.table_ref, bf16[4,16,8,4096]{3,2,1,0:T(8,128)(2,1)} %all-to-all-done.2.point_ref), custom_call_target="tpu_custom_call" | custom-call | flops 4294967296 | bytes 16777216 | tf_op jit(solution)/shard_map/finish/pallas_call | solution.py:430
  (32 shorter events, 0.8 us)
Async XLA Ops:
  9.1 27.5 %copy-start = (bf16[2,128,64]{2,1,0:T(8,128)(2,1)S(1)}, bf16[2,128,64]{2,1,0:T(8,128)(2,1)}, u32[]{:S(2)}) copy-start(bf16[2,128,64]{2,1,0:T(8,128)(2,1)} %constant.77.clone.part_ref) | copy-start | bytes 98308
  9.1 27.5 %copy-start.2 = (bf16[2,64,128]{2,1,0:T(8,128)(2,1)S(1)}, bf16[2,64,128]{2,1,0:T(8,128)(2,1)}, u32[]{:S(2)}) copy-start(bf16[2,64,128]{2,1,0:T(8,128)(2,1)} %constant.78.clone.pack_ref) | copy-start | bytes 98308
  9.1 27.5 %copy-start.4 = (bf16[128,128]{1,0:T(8,128)(2,1)S(1)}, bf16[128,128]{1,0:T(8,128)(2,1)}, u32[]{:S(2)}) copy-start(bf16[128,128]{1,0:T(8,128)(2,1)} %constant.75.clone.turn_ref) | copy-start | bytes 98308
  9.1 27.5 %copy-start.5 = (bf16[32,512]{1,0:T(8,128)(2,1)S(1)}, bf16[32,512]{1,0:T(8,128)(2,1)}, u32[]{:S(2)}) copy-start(bf16[32,512]{1,0:T(8,128)(2,1)} %constant.73.clone.lines_ref) | copy-start | bytes 98308
  36.7 25.8 %copy-start.1 = (bf16[256,64]{1,0:T(8,128)(2,1)S(1)}, bf16[256,64]{1,0:T(8,128)(2,1)}, u32[]{:S(2)}) copy-start(bf16[256,64]{1,0:T(8,128)(2,1)} %constant.74.clone.lines_ref) | copy-start | bytes 98308
  36.7 25.8 %copy-start.3 = (bf16[128,128]{1,0:T(8,128)(2,1)S(1)}, bf16[128,128]{1,0:T(8,128)(2,1)}, u32[]{:S(2)}) copy-start(bf16[128,128]{1,0:T(8,128)(2,1)} %constant.76.clone.turn_ref) | copy-start | bytes 98308
  53.9 17.2 %copy-start.9 = (bf16[64]{0:T(256)(128)(2,1)S(1)}, bf16[64]{0:T(256)(128)(2,1)}, u32[]{:S(2)}) copy-start(bf16[64]{0:T(256)(128)(2,1)} %param.17) | copy-start | bytes 388
  65.6 29.2 %all-to-all-start = ((bf16[32,16,8,128]{3,2,1,0:T(8,128)(2,1)}), bf16[32,16,8,128]{3,2,1,0:T(8,128)(2,1)S(1)}, u32[]{:S(2)}, u32[]{:S(2)}) async-start(bf16[32,16,8,128]{3,2,1,0:T(8,128)(2,1)} %bitcast.8), calls=%async_computation | async-start | bytes 2097152 | tf_op jit(solution)/shard_map/all_to_all | solution.py:635
  71.3 23.8 %copy-start.6 = (bf16[64,64]{1,0:T(8,128)(2,1)S(1)}, bf16[64,64]{1,0:T(8,128)(2,1)}, u32[]{:S(2)}) copy-start(bf16[64,64]{1,0:T(8,128)(2,1)} %point_weight_ref.1) | copy-start | bytes 24580
  71.3 23.8 %copy-start.7 = (bf16[512,64]{1,0:T(8,128)(2,1)S(1)}, bf16[512,64]{1,0:T(8,128)(2,1)}, u32[]{:S(2)}) copy-start(bf16[512,64]{1,0:T(8,128)(2,1)} %constant.79.clone.repeat_ref) | copy-start | bytes 196612
  215.3 53.8 %all-to-all-start.2 = ((bf16[4,16,8,4096]{3,2,1,0:T(8,128)(2,1)}), bf16[4,16,8,4096]{3,2,1,0:T(8,128)(2,1)}, u32[]{:S(2)}, u32[]{:S(2)}) async-start(bf16[4,16,8,4096]{3,2,1,0:T(8,128)(2,1)} %bitcast.60), calls=%async_computation.2 | async-start | bytes 8388608 | tf_op jit(solution)/shard_map/all_to_all | solution.py:659
  222.3 12.2 %copy-start.8 = (bf16[8,16,32,128]{3,2,1,0:T(8,128)(2,1)S(1)}, bf16[8,16,32,128]{3,2,1,0:T(8,128)(2,1)}, u32[]{:S(2)}) copy-start(bf16[8,16,32,128]{3,2,1,0:T(8,128)(2,1)} %all_to_all.15) | copy-start | bytes 3145732

commit v3 on v2

--- a/solution.py
+++ b/solution.py
@@ -307,7 +307,7 @@
 
 
 def grid_kernel(
-    modes_ref, table_ref, field_ref, cotangent_ref, point_weight_ref, repeat_ref, bias_ref,
+    chan_ref, modes_ref, table_ref, field_ref, cotangent_ref, point_weight_ref, repeat_ref, bias_ref,
     point_ref, hat_ref, sums_ref, total, weight_total, bias_total, mix_ref, back_ref, *, planes,
 ):
     step = pl.program_id(0)
@@ -330,13 +330,14 @@
         mix_ref[...] = back.T.astype(jnp.bfloat16)
 
     table = table_ref[...]
-    field = field_ref[...]
+    shape = (rows, field_ref.shape[-1])
+    field = field_ref[...].astype(jnp.float32).reshape(shape).astype(jnp.bfloat16)
     pre_act = lax.dot_general(
         modes_ref[...], table, ROWS_BY_ROWS, preferred_element_type=jnp.float32
     )
     pre_act += jnp.dot(mix_ref[...], field, preferred_element_type=jnp.float32)
     pre_act += bias_ref[...]
-    grad_wide = cotangent_ref[...].astype(jnp.float32) * gelu_grad(pre_act)
+    grad_wide = cotangent_ref[...].astype(jnp.float32).reshape(shape) * gelu_grad(pre_act)
     grad_pre = grad_wide.astype(jnp.bfloat16)
     point_ref[...] = jnp.dot(
         back_ref[...], grad_pre, preferred_element_type=jnp.float32
@@ -369,41 +370,45 @@
         )
 
 
-def grid_stage(modes, table, field, cotangent, point_weight, bias, planes, parts):
+def grid_stage(chan_index, modes, table, field, cotangent, point_weight, bias, parts):
     rows, width = modes.shape
     cells = table.shape[0]
     channels = point_weight.shape[0]
+    planes = rows // channels
     block = pick(cells, 512)
-    along = lambda s: (0, s)
     repeat = jnp.asarray(np.repeat(np.eye(channels, dtype=np.float32), planes, 0).astype(BF16))
+    own = pl.BlockSpec((channels, planes, block), lambda s, chan: (0, chan[0], s))
     return pl.pallas_call(
         functools.partial(grid_kernel, planes=planes),
-        grid=(cells // block,),
-        in_specs=[
-            whole((rows, width)),
-            pl.BlockSpec((block, width), lambda s: (s, 0)),
-            pl.BlockSpec((rows, block), along),
-            pl.BlockSpec((rows, block), along),
-            whole((channels, channels)),
-            whole((rows, channels)),
-            whole((rows, 1)),
-        ],
-        out_specs=[
-            pl.BlockSpec((rows, block), along),
-            whole((parts, rows, width // parts)),
-            whole((channels + 8, channels)),
-        ],
+        grid_spec=pltpu.PrefetchScalarGridSpec(
+            num_scalar_prefetch=1,
+            grid=(cells // block,),
+            in_specs=[
+                whole((rows, width)),
+                pl.BlockSpec((block, width), lambda s, chan: (s, 0)),
+                own,
+                own,
+                whole((channels, channels)),
+                whole((rows, channels)),
+                whole((rows, 1)),
+            ],
+            out_specs=[
+                pl.BlockSpec((rows, block), lambda s, chan: (0, s)),
+                whole((parts, rows, width // parts)),
+                whole((channels + 8, channels)),
+            ],
+            scratch_shapes=[
+                pltpu.VMEM((rows, width), jnp.float32),
+                pltpu.VMEM((rows, rows), jnp.float32),
+                pltpu.VMEM((rows, 1), jnp.float32),
+                pltpu.VMEM((rows, rows), jnp.bfloat16),
+                pltpu.VMEM((rows, rows), jnp.bfloat16),
+            ],
+        ),
         out_shape=[
             jax.ShapeDtypeStruct((rows, cells), jnp.bfloat16),
             jax.ShapeDtypeStruct((parts, rows, width // parts), jnp.bfloat16),
             jax.ShapeDtypeStruct((channels + 8, channels), jnp.float32),
-        ],
-        scratch_shapes=[
-            pltpu.VMEM((rows, width), jnp.float32),
-            pltpu.VMEM((rows, rows), jnp.float32),
-            pltpu.VMEM((rows, 1), jnp.float32),
-            pltpu.VMEM((rows, rows), jnp.bfloat16),
-            pltpu.VMEM((rows, rows), jnp.bfloat16),
         ],
         compiler_params=params(),
         cost_estimate=pl.CostEstimate(
@@ -412,7 +417,7 @@
             transcendentals=2 * rows * cells,
         ),
         name="grid",
-    )(modes, table, field, cotangent, point_weight, repeat, bias)
+    )(chan_index.reshape(1), modes, table, field, cotangent, point_weight, repeat, bias)
 
 
 def finish_kernel(modes_ref, table_ref, point_ref, out_ref):
@@ -632,28 +637,28 @@
     pencils = pencils.reshape(group, slabs, chans, own_planes, width)
     pencils = jnp.transpose(pencils, (1, 2, 0, 3, 4))
     pencils = pencils.reshape(slabs * chans, group, own_planes, width)
-    slabs_in = lax.all_to_all(
-        pencils, ("slab", "chan"), split_axis=0, concat_axis=0, tiled=True
-    )
+    (slabs_in,) = exchange([pencils], *everyone, 4)
     slabs_in = slabs_in.reshape(slabs, channels, own_planes, width)
     rows = channels * own_planes
     slabs_in = jnp.transpose(slabs_in, (1, 2, 0, 3)).reshape(rows, slabs * width)
 
-    first_plane = chan_index * own_planes
-    plane_field = lax.dynamic_slice_in_dim(
-        pad_planes(field, 1, spare), first_plane, own_planes, 1
-    )
-    plane_cotangent = lax.dynamic_slice_in_dim(
-        pad_planes(cotangent, 1, spare), first_plane, own_planes, 1
-    )
+    own_index, own_field, own_cotangent = chan_index, field, cotangent
+    if not tiled:
+        own_index = jnp.zeros_like(chan_index)
+        own_field, own_cotangent = (
+            lax.dynamic_slice_in_dim(
+                pad_planes(array, 1, spare), chan_index * own_planes, own_planes, 1
+            )
+            for array in (field, cotangent)
+        )
     point, hat_rows, sums = grid_stage(
+        own_index,
         slabs_in,
         table,
-        plane_field.reshape(rows, cells),
-        plane_cotangent.reshape(rows, cells),
+        own_field,
+        own_cotangent,
         point_weight,
         jnp.repeat(point_bias.astype(jnp.float32), own_planes)[:, None],
-        own_planes,
         slabs if tiled else 1,
     )
     point = lax.all_to_all(
@@ -676,9 +681,8 @@
         hat.reshape(channels, MX, width), lines_back, turn_back, part, pack, weight
     )
     pencils = pencils.reshape(group, slabs, planes, width)
-    pencils = lax.all_to_all(
-        jnp.moveaxis(pencils, 1, 0), "slab", split_axis=0, concat_axis=0, tiled=True
-    )
+    pencils, point = lax.optimization_barrier((pencils, point))
+    (pencils,) = exchange([jnp.moveaxis(pencils, 1, 0)], ("slab",), (slabs,), 5)
     grad_spectral = jnp.swapaxes(outer(coeff, hat), 3, 4)
     pencils = jnp.moveaxis(pencils, 0, 2).reshape(group * planes, slabs * width)
     if tiled:

time: 284 us -> 267 us (0.940); the launches traced: 280 us -> 266 us
  Pallas kernels: 179 us -> 256 us
  waiting for transfers between devices: 49.1 us -> 0.01 us
  blocking collectives: 27.1 us -> 0 us
  local copies, waits for them, and re-layouts: 12.3 us -> 3.86 us
  starting transfers between devices: 11.8 us -> 4.86 us
    pallas_call x4 -> x6, Pallas kernels: 85 us -> 163 us  [exchange(): pl.pallas_call(functools.partial(exchange_kernel, axes, sizes, blocks), i...]
    all_to_all x1, waiting for transfers between devices: 33.6 us -> 0.01 us  [body(): lax.all_to_all(point.reshape(chans, group, own_planes, cells), 'chan', sp...]
    all_to_all x1 -> x0, blocking collectives: 27.1 us -> none  [body(): lax.all_to_all(jnp.moveaxis(pencils, 1, 0), 'slab', split_axis=0, concat_...]
    all_to_all x1 -> x0, waiting for transfers between devices: 15.5 us -> none  [body(): lax.all_to_all(pencils, ('slab', 'chan'), split_axis=0, concat_axis=0, ti...]
    reshape x2 -> x1, local copies, waits for them, and re-layouts: 8.1 us -> 0.15 us  [body(): jnp.transpose(slabs_in, (1, 2, 0, 3)).reshape(rows, slabs * width)]
    all_to_all x1 -> x0, starting transfers between devices: 5.46 us -> none  [body(): lax.all_to_all(pencils, ('slab', 'chan'), split_axis=0, concat_axis=0, ti...]
  transfers between devices with their start and end apart: 2 -> 1, of which waited for: 2 -> 0; matrix products, arithmetic and copies ran while one was open for 4% -> 1% of each run, Pallas kernels for 4% -> 39%
where the time goes in v3:
time: 267 us; the launch traced here: 266 us
  Pallas kernels  256 us (96%)
  starting transfers between devices  4.86 us (2%)
  local copies, waits for them, and re-layouts  3.86 us (1%)
    pallas_call x6, Pallas kernels, exchange(): pl.pallas_call(functools.partial(exchange_kernel, axes, sizes, blocks), i...  163 us
    pallas_call x1, Pallas kernels, grid_stage(): pl.pallas_call(functools.partial(grid_kernel, planes=planes), grid_spec=p...  25.1 us
    pallas_call x1, Pallas kernels, mix(): pl.pallas_call(functools.partial(mix_kernel, inner=pick(block, 4)), grid=...  17.2 us
    pallas_call x1, Pallas kernels, adjoint_of(): pl.pallas_call(adjoint_kernel, grid=(group // block,), in_specs=[whole(ha...  16.7 us
    pallas_call x1, Pallas kernels, outer(): pl.pallas_call(outer_kernel, grid=(group // block,), in_specs=[pl.BlockSp...  11.7 us
    pallas_call x1, Pallas kernels, finish(): pl.pallas_call(finish_kernel, grid=(cells // block,), in_specs=[whole((ro...  10.9 us
    pallas_call x1, Pallas kernels, begin(): pl.pallas_call(begin_kernel, grid_spec=pltpu.PrefetchScalarGridSpec(num_s...  8.46 us
  transfers between devices with their start and end apart: 1, of which 0 were waited for; matrix products, arithmetic and copies ran while one was open for 1% of the time, Pallas kernels for 39%

profile of v3, /device:TPU:13, one launch (start us, length us, event | category | flops | bytes accessed | tf_op | source)
XLA Modules:
  0.0 266.1 jit_solution(2729478798696775265)
XLA Ops:
  0.7 0.7 broadcast_in_dim.23
  1.4 0.1 broadcast_in_dim_reshape.4.bias_ref
  1.6 8.5 %begin.1.refs_0_ = bf16[8,512,128]{2,1,0:T(8,128)(2,1)S(1)} custom-call(s32[1]{0:T(128)} %bitcast.chan_ref, bf16[64,32,4096]{2,1,0:T(8,128)(2,1)} %field_ref.3, bf16[4096,1024]{1,0:T(8,128)(2,1)} %constant.68.clone.table_ref), custom_call_target="tpu_custom_call" | custom-call | flops 4294967296 | bytes 12582912 | tf_op jit(solution)/shard_map/begin/pallas_call | solution.py:480
  10.0 27.3 %exchange.6 = bf16[8,512,128]{2,1,0:T(8,128)(2,1)S(1)} custom-call(bf16[8,512,128]{2,1,0:T(8,128)(2,1)S(1)} %begin.1.refs_0_), custom_call_target="tpu_custom_call" | custom-call | bytes 8388608 | tf_op jit(solution)/shard_map/exchange/pallas_call | solution.py:572
  37.6 17.2 %mix.1 = (bf16[64,32,128]{2,1,0:T(8,128)(2,1)S(1)}, f32[16,2,32,64]{3,2,1,0:T(8,128)S(1)}) custom-call(bf16[16,256,128]{2,1,0:T(8,128)(2,1)S(1)} %bitcast.43, bf16[32,512]{1,0:T(8,128)(2,1)S(1)} %copy-done.5, bf16[128,128]{1,0:T(8,128)(2,1)S(1)} %copy-done.4, bf16[2,128,64]{2,1,0:T(8,128)(2,1)S(1)} %copy-done, bf16[2,64,128]{2,1,0:T(8,128)(2,1)S(1)} %copy-done.2, ...), custom_call_target="tpu_custom_call" | custom-call | flops 16777216 | bytes 16777216 | tf_op jit(solution)/shard_map/mix/pallas_call | solution.py:142
  54.8 8.6 %exchange.7.parts_ref = bf16[4,16,32,128]{3,2,1,0:T(8,128)(2,1)S(1)} custom-call(bf16[4,16,32,128]{3,2,1,0:T(8,128)(2,1)S(1)} %bitcast.57), custom_call_target="tpu_custom_call" | custom-call | bytes 4194304 | tf_op jit(solution)/shard_map/exchange/pallas_call | solution.py:572
  63.4 1.9 spread.1
  65.3 0.3 copy.23
  65.6 28.3 %exchange.8 = bf16[32,16,8,128]{3,2,1,0:T(8,128)(2,1)S(1)} custom-call(bf16[32,16,8,128]{3,2,1,0:T(8,128)(2,1)S(1)} %bitcast.48), custom_call_target="tpu_custom_call" | custom-call | bytes 8388608 | tf_op jit(solution)/shard_map/exchange/pallas_call | solution.py:572
  93.8 0.1 copy_bitcast_fusion.2.modes_ref
  94.0 25.1 %grid.1 = (bf16[512,4096]{1,0:T(8,128)(2,1)}, bf16[8,512,128]{2,1,0:T(8,128)(2,1)S(1)}, f32[72,64]{1,0:T(8,128)S(1)}) custom-call(s32[1]{0:T(128)} %bitcast.chan_ref, bf16[512,1024]{1,0:T(8,128)(2,1)S(1)} %copy_bitcast_fusion.2.modes_ref, bf16[4096,1024]{1,0:T(8,128)(2,1)} %constant.68.clone.table_ref, bf16[64,32,4096]{2,1,0:T(8,128)(2,1)} %field_ref.3, ...), custom_call_target="tpu_custom_call" | custom-call | flops 15032385536 | bytes 20971520 | tf_op jit(solution)/shard_map/grid/pallas_call | solution.py:381
  119.1 4.9 %all-to-all-start = ((bf16[4,16,8,4096]{3,2,1,0:T(8,128)(2,1)}), bf16[4,16,8,4096]{3,2,1,0:T(8,128)(2,1)}, u32[]{:S(2)}, u32[]{:S(2)}) async-start(bf16[4,16,8,4096]{3,2,1,0:T(8,128)(2,1)} %bitcast.62), calls=%async_computation | async-start | bytes 8388608 | tf_op jit(solution)/shard_map/all_to_all | solution.py:664
  124.1 64.5 %exchange.9 = (bf16[32,16,8,128]{3,2,1,0:T(8,128)(2,1)S(1)}, f32[32,24,64]{2,1,0:T(8,128)S(1)}) custom-call(bf16[32,16,8,128]{3,2,1,0:T(8,128)(2,1)S(1)} %bitcast.53, f32[4,24,64]{2,1,0:T(8,128)S(1)} %pad_maximum_fusion.refs_1_), custom_call_target="tpu_custom_call" | custom-call | bytes 8486912 | tf_op jit(solution)/shard_map/exchange/pallas_call | solution.py:572
  188.6 0.3 copy.26
  188.9 1.6 lines.1
  190.5 0.6 slice.16
  191.1 8.1 %exchange.10 = bf16[4,16,32,128]{3,2,1,0:T(8,128)(2,1)S(1)} custom-call(bf16[1,16,32,128]{3,2,1,0:T(8,128)(2,1)S(1)} %bitcast.56), custom_call_target="tpu_custom_call" | custom-call | bytes 1048576 | tf_op jit(solution)/shard_map/exchange/pallas_call | solution.py:572
  199.3 16.7 %adjoint.1 = (bf16[16,256,128]{2,1,0:T(8,128)(2,1)S(1)}, f32[64,2,32,64]{3,2,1,0:T(8,128)S(1)}) custom-call(bf16[64,32,128]{2,1,0:T(8,128)(2,1)S(1)} %bitcast.52, bf16[256,64]{1,0:T(8,128)(2,1)S(1)} %copy-done.1, bf16[128,128]{1,0:T(8,128)(2,1)S(1)} %copy-done.3, bf16[2,128,64]{2,1,0:T(8,128)(2,1)S(1)} %copy-done, bf16[2,64,128]{2,1,0:T(8,128)(2,1)S(1)} %copy-done.2, ...), custom_call_target="tpu_custom_call" | custom-call | flops 16777216 | bytes 16777216 | tf_op jit(solution)/shard_map/adjoint/pallas_call | solution.py:245
  216.0 11.7 %outer.1 = f32[2,16,64,32,64]{4,3,2,1,0:T(8,128)} custom-call(f32[16,2,32,64]{3,2,1,0:T(8,128)S(1)} %get-tuple-element.23.coeff_ref, f32[64,2,32,64]{3,2,1,0:T(8,128)S(1)} %get-tuple-element.24.hat_ref), custom_call_target="tpu_custom_call" | custom-call | flops 12582912 | bytes 33554432 | tf_op jit(solution)/shard_map/outer/pallas_call | solution.py:287
  227.7 0.5 slice_bitcast_fusion
  228.3 25.9 %exchange.11 = bf16[8,16,32,128]{3,2,1,0:T(8,128)(2,1)S(1)} custom-call(bf16[8,16,32,128]{3,2,1,0:T(8,128)(2,1)S(1)} %bitcast.50), custom_call_target="tpu_custom_call" | custom-call | bytes 8388608 | tf_op jit(solution)/shard_map/exchange/pallas_call | solution.py:572
  254.2 0.7 copy.28
  254.9 0.3 copy.33
  255.2 10.9 %finish.1 = bf16[512,4096]{1,0:T(8,128)(2,1)} custom-call(bf16[512,1024]{1,0:T(8,128)(2,1)S(1)} %bitcast.44, bf16[4096,1024]{1,0:T(8,128)(2,1)} %constant.68.clone.table_ref, bf16[4,16,8,4096]{3,2,1,0:T(8,128)(2,1)} %all-to-all-done.point_ref), custom_call_target="tpu_custom_call" | custom-call | flops 4294967296 | bytes 16777216 | tf_op jit(solution)/shard_map/finish/pallas_call | solution.py:435
  (26 shorter events, 0.3 us)
Async XLA Ops:
  1.5 36.0 %copy-start = (bf16[2,128,64]{2,1,0:T(8,128)(2,1)S(1)}, bf16[2,128,64]{2,1,0:T(8,128)(2,1)}, u32[]{:S(2)}) copy-start(bf16[2,128,64]{2,1,0:T(8,128)(2,1)} %constant.73.clone.part_ref) | copy-start | bytes 98308
  1.5 36.0 %copy-start.2 = (bf16[2,64,128]{2,1,0:T(8,128)(2,1)S(1)}, bf16[2,64,128]{2,1,0:T(8,128)(2,1)}, u32[]{:S(2)}) copy-start(bf16[2,64,128]{2,1,0:T(8,128)(2,1)} %constant.74.clone.pack_ref) | copy-start | bytes 98308
  1.5 36.0 %copy-start.4 = (bf16[128,128]{1,0:T(8,128)(2,1)S(1)}, bf16[128,128]{1,0:T(8,128)(2,1)}, u32[]{:S(2)}) copy-start(bf16[128,128]{1,0:T(8,128)(2,1)} %constant.71.clone.turn_ref) | copy-start | bytes 98308
  1.6 36.0 %copy-start.5 = (bf16[32,512]{1,0:T(8,128)(2,1)S(1)}, bf16[32,512]{1,0:T(8,128)(2,1)}, u32[]{:S(2)}) copy-start(bf16[32,512]{1,0:T(8,128)(2,1)} %constant.69.clone.lines_ref) | copy-start | bytes 98308
  37.5 25.8 %copy-start.1 = (bf16[256,64]{1,0:T(8,128)(2,1)S(1)}, bf16[256,64]{1,0:T(8,128)(2,1)}, u32[]{:S(2)}) copy-start(bf16[256,64]{1,0:T(8,128)(2,1)} %constant.70.clone.lines_ref) | copy-start | bytes 98308
  37.6 25.8 %copy-start.3 = (bf16[128,128]{1,0:T(8,128)(2,1)S(1)}, bf16[128,128]{1,0:T(8,128)(2,1)}, u32[]{:S(2)}) copy-start(bf16[128,128]{1,0:T(8,128)(2,1)} %constant.72.clone.turn_ref) | copy-start | bytes 98308
  54.8 39.2 %copy-start.6 = (bf16[64,64]{1,0:T(8,128)(2,1)S(1)}, bf16[64,64]{1,0:T(8,128)(2,1)}, u32[]{:S(2)}) copy-start(bf16[64,64]{1,0:T(8,128)(2,1)} %point_weight_ref.1) | copy-start | bytes 24580
  54.8 39.2 %copy-start.7 = (bf16[512,64]{1,0:T(8,128)(2,1)S(1)}, bf16[512,64]{1,0:T(8,128)(2,1)}, u32[]{:S(2)}) copy-start(bf16[512,64]{1,0:T(8,128)(2,1)} %constant.75.clone.repeat_ref) | copy-start | bytes 196612
  119.1 109.1 %all-to-all-start = ((bf16[4,16,8,4096]{3,2,1,0:T(8,128)(2,1)}), bf16[4,16,8,4096]{3,2,1,0:T(8,128)(2,1)}, u32[]{:S(2)}, u32[]{:S(2)}) async-start(bf16[4,16,8,4096]{3,2,1,0:T(8,128)(2,1)} %bitcast.62), calls=%async_computation | async-start | bytes 8388608 | tf_op jit(solution)/shard_map/all_to_all | solution.py:664

commit v4 on v3

--- a/solution.py
+++ b/solution.py
@@ -420,27 +420,36 @@
     )(chan_index.reshape(1), modes, table, field, cotangent, point_weight, repeat, bias)
 
 
-def finish_kernel(modes_ref, table_ref, point_ref, out_ref):
+def finish_kernel(chan_ref, modes_ref, table_ref, *refs):
+    *point_refs, out_ref, point = refs
+    chans = len(point_refs)
+    for shift, point_ref in enumerate(point_refs):
+        sender = lax.rem(chan_ref[0] + chans - shift, chans)
+        point[sender] = point_ref[...].astype(jnp.float32).reshape(point.shape[1:])
     back = lax.dot_general(
         modes_ref[...], table_ref[...], ROWS_BY_ROWS, preferred_element_type=jnp.float32
     )
-    point = jnp.swapaxes(point_ref[...].astype(jnp.float32), 0, 1)
-    out_ref[...] = (back + point.reshape(back.shape)).astype(out_ref.dtype)
-
-
-def finish(modes, table, point):
-    chans, group, planes, cells = point.shape
+    sums = back + jnp.swapaxes(point[...], 0, 1).reshape(back.shape)
+    out_ref[...] = sums.astype(out_ref.dtype)
+
+
+def finish(chan_index, modes, table, points):
+    group, planes, cells = points[0].shape
+    chans = len(points)
     rows, width = modes.shape
     block = pick(cells, 512)
     return pl.pallas_call(
         finish_kernel,
-        grid=(cells // block,),
-        in_specs=[
-            whole((rows, width)),
-            pl.BlockSpec((block, width), lambda s: (s, 0)),
-            pl.BlockSpec((chans, group, planes, block), lambda s: (0, 0, 0, s)),
-        ],
-        out_specs=pl.BlockSpec((rows, block), lambda s: (0, s)),
+        grid_spec=pltpu.PrefetchScalarGridSpec(
+            num_scalar_prefetch=1,
+            grid=(cells // block,),
+            in_specs=[
+                whole((rows, width)),
+                pl.BlockSpec((block, width), lambda s, chan: (s, 0)),
+            ] + [pl.BlockSpec((group, planes, block), lambda s, chan: (0, 0, s))] * chans,
+            out_specs=pl.BlockSpec((rows, block), lambda s, chan: (0, s)),
+            scratch_shapes=[pltpu.VMEM((chans, group, planes, block), jnp.float32)],
+        ),
         out_shape=jax.ShapeDtypeStruct((rows, cells), jnp.bfloat16),
         compiler_params=params(),
         cost_estimate=pl.CostEstimate(
@@ -449,7 +458,7 @@
             transcendentals=0,
         ),
         name="finish",
-    )(modes, table, point)
+    )(chan_index.reshape(1), modes, table, *points)
 
 
 def begin_kernel(chan_ref, field_ref, table_ref, out_ref, total):
@@ -585,7 +594,7 @@
             collective_id=collective_id, has_side_effects=True, vmem_limit_bytes=VMEM_LIMIT
         ),
         cost_estimate=pl.CostEstimate(
-            flops=0, bytes_accessed=sum(8 * 2 * a.size for a in arrays), transcendentals=0
+            flops=0, bytes_accessed=sum(2 * a.size for a in arrays), transcendentals=0
         ),
         name="exchange",
     )(*arrays)
@@ -661,10 +670,6 @@
         jnp.repeat(point_bias.astype(jnp.float32), own_planes)[:, None],
         slabs if tiled else 1,
     )
-    point = lax.all_to_all(
-        point.reshape(chans, group, own_planes, cells),
-        "chan", split_axis=0, concat_axis=0, tiled=True,
-    )
     if not tiled:
         hat_rows = jnp.moveaxis(hat_rows.reshape(rows, slabs, width), 1, 0)
     hat_rows = hat_rows.reshape(slabs * chans, group, own_planes, width)
@@ -676,20 +681,30 @@
     pencils = pencils.reshape(group, slabs, chans * own_planes, width)[:, :, :planes]
     part_hat = gather_lines(pencils.reshape(group, length, width), scale, lines, turn)
     (hat,) = exchange([part_hat[None]], ("chan",), (chans,), 3)
+    hat, point = lax.optimization_barrier((hat, point))
+    point = point.reshape(chans, group, own_planes, cells)
+    points = []
+    for shift in range(chans):
+        receiver = (chan_index + shift) % chans
+        block = lax.dynamic_index_in_dim(point, receiver, 0, keepdims=False)
+        if shift:
+            block = lax.ppermute(block, "chan", [(c, (c + shift) % chans) for c in range(chans)])
+        points.append(block)
 
     pencils, hat = adjoint_of(
         hat.reshape(channels, MX, width), lines_back, turn_back, part, pack, weight
     )
     pencils = pencils.reshape(group, slabs, planes, width)
-    pencils, point = lax.optimization_barrier((pencils, point))
     (pencils,) = exchange([jnp.moveaxis(pencils, 1, 0)], ("slab",), (slabs,), 5)
     grad_spectral = jnp.swapaxes(outer(coeff, hat), 3, 4)
     pencils = jnp.moveaxis(pencils, 0, 2).reshape(group * planes, slabs * width)
     if tiled:
-        grad_input = finish(pencils, table, point).reshape(group, planes, cells)
+        grad_input = finish(chan_index, pencils, table, points).reshape(group, planes, cells)
     else:
         back = lax.dot_general(pencils, table, ROWS_BY_ROWS, preferred_element_type=jnp.float32)
         back = back.reshape(group, planes, cells)
+        order = (chan_index - jnp.arange(chans)) % chans
+        point = jnp.take(jnp.stack(points), order, axis=0)
         point = jnp.moveaxis(point, 0, 1).reshape(group, chans * own_planes, cells)[:, :planes]
         grad_input = (back + point.astype(jnp.float32)).astype(jnp.bfloat16)
 

time: 267 us -> 247 us (0.925)
  Pallas kernels: 256 us -> 231 us
  local copies, waits for them, and re-layouts: 3.86 us -> 11 us
    pallas_call x6, Pallas kernels: 163 us -> 138 us  [exchange(): pl.pallas_call(functools.partial(exchange_kernel, axes, sizes, blocks), i...]
    all_to_all x1 -> x0, starting transfers between devices: 4.86 us -> none  [body(): lax.all_to_all(point.reshape(chans, group, own_planes, cells), 'chan', sp...]
    squeeze x0 -> x1, local copies, waits for them, and re-layouts: none -> 3.95 us  [body(): block = lax.dynamic_index_in_dim(point, receiver, 0, keepdims=False)]
    ppermute x0 -> x3, starting transfers between devices: none -> 3.31 us  [body(): lax.ppermute(block, 'chan', [(c, (c + shift) % chans) for c in range(chan...]
    unnamed x17 -> x25, local copies, waits for them, and re-layouts: 0.32 us -> 3.51 us
  transfers between devices with their start and end apart: 1 -> 3, of which waited for: 0 -> 0; matrix products, arithmetic and copies ran while one was open for 1% -> 1% of each run, Pallas kernels for 39% -> 22%
where the time goes in v4:
time: 247 us; the launch traced here: 246 us
  Pallas kernels  231 us (94%)
  local copies, waits for them, and re-layouts  11 us (4%)
  starting transfers between devices  3.31 us (1%)
    pallas_call x6, Pallas kernels, exchange(): pl.pallas_call(functools.partial(exchange_kernel, axes, sizes, blocks), i...  138 us
    pallas_call x1, Pallas kernels, grid_stage(): pl.pallas_call(functools.partial(grid_kernel, planes=planes), grid_spec=p...  25.1 us
    pallas_call x1, Pallas kernels, mix(): pl.pallas_call(functools.partial(mix_kernel, inner=pick(block, 4)), grid=...  17.2 us
    pallas_call x1, Pallas kernels, adjoint_of(): pl.pallas_call(adjoint_kernel, grid=(group // block,), in_specs=[whole(ha...  16.7 us
    pallas_call x1, Pallas kernels, outer(): pl.pallas_call(outer_kernel, grid=(group // block,), in_specs=[pl.BlockSp...  11.7 us
    pallas_call x1, Pallas kernels, finish(): pl.pallas_call(finish_kernel, grid_spec=pltpu.PrefetchScalarGridSpec(num_...  10.6 us
    pallas_call x1, Pallas kernels, begin(): pl.pallas_call(begin_kernel, grid_spec=pltpu.PrefetchScalarGridSpec(num_s...  8.46 us
  transfers between devices with their start and end apart: 3, of which 0 were waited for; matrix products, arithmetic and copies ran while one was open for 1% of the time, Pallas kernels for 22%

profile of v4, /device:TPU:13, one launch (start us, length us, event | category | flops | bytes accessed | tf_op | source)
XLA Modules:
  0.0 246.5 jit_solution(2819767292608555283)
XLA Ops:
  0.7 0.7 broadcast_in_dim.23
  1.6 8.5 %begin.1.refs_0_ = bf16[8,512,128]{2,1,0:T(8,128)(2,1)S(1)} custom-call(s32[1]{0:T(128)} %bitcast.chan_ref, bf16[64,32,4096]{2,1,0:T(8,128)(2,1)} %field_ref.3, bf16[4096,1024]{1,0:T(8,128)(2,1)} %constant.106.clone.table_ref), custom_call_target="tpu_custom_call" | custom-call | flops 4294967296 | bytes 12582912 | tf_op jit(solution)/shard_map/begin/pallas_call | solution.py:489
  10.1 27.3 %exchange.6 = bf16[8,512,128]{2,1,0:T(8,128)(2,1)S(1)} custom-call(bf16[8,512,128]{2,1,0:T(8,128)(2,1)S(1)} %begin.1.refs_0_), custom_call_target="tpu_custom_call" | custom-call | bytes 1048576 | tf_op jit(solution)/shard_map/exchange/pallas_call | solution.py:581
  37.6 17.2 %mix.1 = (bf16[64,32,128]{2,1,0:T(8,128)(2,1)S(1)}, f32[16,2,32,64]{3,2,1,0:T(8,128)S(1)}) custom-call(bf16[16,256,128]{2,1,0:T(8,128)(2,1)S(1)} %bitcast.52, bf16[32,512]{1,0:T(8,128)(2,1)S(1)} %copy-done.9, bf16[128,128]{1,0:T(8,128)(2,1)S(1)} %copy-done.8, bf16[2,128,64]{2,1,0:T(8,128)(2,1)S(1)} %copy-done, bf16[2,64,128]{2,1,0:T(8,128)(2,1)S(1)} %copy-done.4, ...), custom_call_target="tpu_custom_call" | custom-call | flops 16777216 | bytes 16777216 | tf_op jit(solution)/shard_map/mix/pallas_call | solution.py:142
  54.8 8.6 %exchange.7.parts_ref = bf16[4,16,32,128]{3,2,1,0:T(8,128)(2,1)S(1)} custom-call(bf16[4,16,32,128]{3,2,1,0:T(8,128)(2,1)S(1)} %bitcast.65), custom_call_target="tpu_custom_call" | custom-call | bytes 524288 | tf_op jit(solution)/shard_map/exchange/pallas_call | solution.py:581
  63.5 1.9 spread.1
  65.6 28.3 %exchange.8 = bf16[32,16,8,128]{3,2,1,0:T(8,128)(2,1)S(1)} custom-call(bf16[32,16,8,128]{3,2,1,0:T(8,128)(2,1)S(1)} %bitcast.56), custom_call_target="tpu_custom_call" | custom-call | bytes 1048576 | tf_op jit(solution)/shard_map/exchange/pallas_call | solution.py:581
  94.1 25.1 %grid.1 = (bf16[512,4096]{1,0:T(8,128)(2,1)}, bf16[8,512,128]{2,1,0:T(8,128)(2,1)S(1)}, f32[72,64]{1,0:T(8,128)S(1)}) custom-call(s32[1]{0:T(128)} %bitcast.chan_ref, bf16[512,1024]{1,0:T(8,128)(2,1)S(1)} %copy_bitcast_fusion.2.modes_ref, bf16[4096,1024]{1,0:T(8,128)(2,1)} %constant.106.clone.table_ref, bf16[64,32,4096]{2,1,0:T(8,128)(2,1)} %field_ref.3, ...), custom_call_target="tpu_custom_call" | custom-call | flops 15032385536 | bytes 20971520 | tf_op jit(solution)/shard_map/grid/pallas_call | solution.py:381
  119.2 38.4 %exchange.9 = (bf16[32,16,8,128]{3,2,1,0:T(8,128)(2,1)S(1)}, f32[32,24,64]{2,1,0:T(8,128)S(1)}) custom-call(bf16[32,16,8,128]{3,2,1,0:T(8,128)(2,1)S(1)} %bitcast.61, f32[4,24,64]{2,1,0:T(8,128)S(1)} %pad_maximum_fusion.refs_1_), custom_call_target="tpu_custom_call" | custom-call | bytes 1060864 | tf_op jit(solution)/shard_map/exchange/pallas_call | solution.py:581
  157.9 1.6 lines.1
  159.5 9.8 %exchange.10 = bf16[4,16,32,128]{3,2,1,0:T(8,128)(2,1)S(1)} custom-call(bf16[1,16,32,128]{3,2,1,0:T(8,128)(2,1)S(1)} %bitcast.64), custom_call_target="tpu_custom_call" | custom-call | bytes 131072 | tf_op jit(solution)/shard_map/exchange/pallas_call | solution.py:581
  169.3 4.0 %dynamic-slice_bitcast_fusion = (bf16[16,8,4096]{2,1,0:T(8,128)(2,1)}, bf16[16,8,4096]{2,1,0:T(8,128)(2,1)}, bf16[16,8,4096]{2,1,0:T(8,128)(2,1)}, bf16[16,8,4096]{2,1,0:T(8,128)(2,1)S(1)}) fusion(bf16[4,16,8,4096]{3,2,1,0:T(8,128)(2,1)} %bitcast.70, s32[]{:T(128)S(6)} %select_n.78, s32[]{:T(128)S(6)} %select_n.76, s32[]{:T(128)S(6)} %select_n.74, ...), kind=kLoop, calls=%fused_computation.3 | loop fusion | bytes 8388624 | tf_op jit(solution)/shard_map/jit(dynamic_index_in_dim)/squeeze | solution.py:689
  173.3 1.3 collective-permute-start.1
  174.6 2.0 collective-permute-start
  176.6 0.6 slice.16
  177.2 0.8 copy-done.1
  178.1 0.8 copy-done.3
  178.9 0.8 copy-done.5
  179.7 0.8 copy-done.7
  180.4 16.7 %adjoint.1 = (bf16[16,256,128]{2,1,0:T(8,128)(2,1)S(1)}, f32[64,2,32,64]{3,2,1,0:T(8,128)S(1)}) custom-call(bf16[64,32,128]{2,1,0:T(8,128)(2,1)S(1)} %bitcast.60, bf16[256,64]{1,0:T(8,128)(2,1)S(1)} %copy-done.3, bf16[128,128]{1,0:T(8,128)(2,1)S(1)} %copy-done.7, bf16[2,128,64]{2,1,0:T(8,128)(2,1)S(1)} %copy-done.1, bf16[2,64,128]{2,1,0:T(8,128)(2,1)S(1)} %copy-done.5, ...), custom_call_target="tpu_custom_call" | custom-call | flops 16777216 | bytes 16777216 | tf_op jit(solution)/shard_map/adjoint/pallas_call | solution.py:245
  197.2 25.5 %exchange.11 = bf16[8,16,32,128]{3,2,1,0:T(8,128)(2,1)S(1)} custom-call(bf16[8,16,32,128]{3,2,1,0:T(8,128)(2,1)S(1)} %bitcast.58), custom_call_target="tpu_custom_call" | custom-call | bytes 1048576 | tf_op jit(solution)/shard_map/exchange/pallas_call | solution.py:581
  222.7 0.7 copy.28
  223.7 11.7 %outer.1 = f32[2,16,64,32,64]{4,3,2,1,0:T(8,128)} custom-call(f32[16,2,32,64]{3,2,1,0:T(8,128)S(1)} %get-tuple-element.23.coeff_ref, f32[64,2,32,64]{3,2,1,0:T(8,128)S(1)} %get-tuple-element.24.hat_ref), custom_call_target="tpu_custom_call" | custom-call | flops 12582912 | bytes 33554432 | tf_op jit(solution)/shard_map/outer/pallas_call | solution.py:287
  235.9 10.6 %finish.1 = bf16[512,4096]{1,0:T(8,128)(2,1)} custom-call(s32[1]{0:T(128)} %bitcast.chan_ref, bf16[512,1024]{1,0:T(8,128)(2,1)S(1)} %bitcast.51, bf16[4096,1024]{1,0:T(8,128)(2,1)} %constant.106.clone.table_ref, bf16[16,8,4096]{2,1,0:T(8,128)(2,1)S(1)} %get-tuple-element.29.refs_0_, bf16[16,8,4096]{2,1,0:T(8,128)(2,1)S(1)} %collective-permute-done.refs_1_, ...), custom_call_target="tpu_custom_call" | custom-call | flops 4294967296 | bytes 16777216 | tf_op jit(solution)/shard_map/finish/pallas_call | solution.py:441
  (39 shorter events, 1.9 us)
Async XLA Ops:
  1.6 36.0 %copy-start = (bf16[2,128,64]{2,1,0:T(8,128)(2,1)S(1)}, bf16[2,128,64]{2,1,0:T(8,128)(2,1)}, u32[]{:S(2)}) copy-start(bf16[2,128,64]{2,1,0:T(8,128)(2,1)} %constant.111.clone.part_ref) | copy-start | bytes 98308
  1.6 36.0 %copy-start.4 = (bf16[2,64,128]{2,1,0:T(8,128)(2,1)S(1)}, bf16[2,64,128]{2,1,0:T(8,128)(2,1)}, u32[]{:S(2)}) copy-start(bf16[2,64,128]{2,1,0:T(8,128)(2,1)} %constant.112.clone.pack_ref) | copy-start | bytes 98308
  1.6 36.0 %copy-start.8 = (bf16[128,128]{1,0:T(8,128)(2,1)S(1)}, bf16[128,128]{1,0:T(8,128)(2,1)}, u32[]{:S(2)}) copy-start(bf16[128,128]{1,0:T(8,128)(2,1)} %constant.109.clone.turn_ref) | copy-start | bytes 98308
  1.6 36.0 %copy-start.9 = (bf16[32,512]{1,0:T(8,128)(2,1)S(1)}, bf16[32,512]{1,0:T(8,128)(2,1)}, u32[]{:S(2)}) copy-start(bf16[32,512]{1,0:T(8,128)(2,1)} %constant.107.clone.lines_ref) | copy-start | bytes 98308
  37.6 25.8 %copy-start.2 = (bf16[256,64]{1,0:T(8,128)(2,1)S(1)}, bf16[256,64]{1,0:T(8,128)(2,1)}, u32[]{:S(2)}) copy-start(bf16[256,64]{1,0:T(8,128)(2,1)} %constant.108.clone.lines_ref) | copy-start | bytes 98308
  37.6 25.8 %copy-start.6 = (bf16[128,128]{1,0:T(8,128)(2,1)S(1)}, bf16[128,128]{1,0:T(8,128)(2,1)}, u32[]{:S(2)}) copy-start(bf16[128,128]{1,0:T(8,128)(2,1)} %constant.110.clone.turn_ref) | copy-start | bytes 98308
  54.8 39.2 %copy-start.10 = (bf16[64,64]{1,0:T(8,128)(2,1)S(1)}, bf16[64,64]{1,0:T(8,128)(2,1)}, u32[]{:S(2)}) copy-start(bf16[64,64]{1,0:T(8,128)(2,1)} %point_weight_ref.1) | copy-start | bytes 24580
  54.8 39.2 %copy-start.11 = (bf16[512,64]{1,0:T(8,128)(2,1)S(1)}, bf16[512,64]{1,0:T(8,128)(2,1)}, u32[]{:S(2)}) copy-start(bf16[512,64]{1,0:T(8,128)(2,1)} %constant.113.clone.repeat_ref) | copy-start | bytes 196612
  173.3 62.6 %collective-permute-start.2 = (bf16[16,8,4096]{2,1,0:T(8,128)(2,1)}, bf16[16,8,4096]{2,1,0:T(8,128)(2,1)}, u32[]{:S(2)}, u32[]{:S(2)}) collective-permute-start(bf16[16,8,4096]{2,1,0:T(8,128)(2,1)} %get-tuple-element.26), channel_id=1, source_target_pairs={{0,3},{1,0},{2,1},{3,2},{4,7},{5,4},{6,5},{7,6},{8,11},{9,8},{10,9... | collective-permute-start | bytes 3145736 | tf_op jit(solution)/shard_map/ppermute | solution.py:691
  173.3 62.6 %collective-permute-start.1 = (bf16[16,8,4096]{2,1,0:T(8,128)(2,1)}, bf16[16,8,4096]{2,1,0:T(8,128)(2,1)}, u32[]{:S(2)}, u32[]{:S(2)}) collective-permute-start(bf16[16,8,4096]{2,1,0:T(8,128)(2,1)} %get-tuple-element.27), channel_id=1, source_target_pairs={{0,2},{1,3},{2,0},{3,1},{4,6},{5,7},{6,4},{7,5},{8,10},{9,11},{10,... | collective-permute-start | bytes 3145736 | tf_op jit(solution)/shard_map/ppermute | solution.py:691
  174.6 61.3 %collective-permute-start = (bf16[16,8,4096]{2,1,0:T(8,128)(2,1)}, bf16[16,8,4096]{2,1,0:T(8,128)(2,1)S(1)}, u32[]{:S(2)}, u32[]{:S(2)}) collective-permute-start(bf16[16,8,4096]{2,1,0:T(8,128)(2,1)} %get-tuple-element.28), channel_id=1, source_target_pairs={{0,1},{1,2},{2,3},{3,0},{4,5},{5,6},{6,7},{7,4},{8,9},{9,10},{10,1... | collective-permute-start | bytes 3145736 | tf_op jit(solution)/shard_map/ppermute | solution.py:691
  177.2 0.8 copy-start.1
  178.1 0.8 copy-start.3
  178.9 0.8 copy-start.5
  179.7 0.8 copy-start.7

commit v5 on v4

--- a/solution.py
+++ b/solution.py
@@ -72,11 +72,20 @@
 
 
 def part_of(modes):
-    matrix = np.zeros((2, 2 * modes, modes), np.float32)
+    matrix = np.zeros((2, 2, modes, 2, modes), np.float32)
     index = np.arange(modes)
-    matrix[0, index, index] = 1.0
-    matrix[1, modes + index, index] = 1.0
-    return matrix.astype(BF16)
+    for part in range(2):
+        matrix[part, part, index, :, index] = 1.0
+    return matrix.reshape(2, 2 * modes, 2 * modes).astype(BF16)
+
+
+def pack_of(modes):
+    matrix = np.zeros((2, 2, 2, modes, 2, modes), np.float32)
+    index = np.arange(modes)
+    for half in range(2):
+        for part in range(2):
+            matrix[half, part, half, index, part, index] = 1.0
+    return matrix.reshape(2, 2, 2 * modes, 2 * modes).astype(BF16)
 
 
 def wide(a, b):
@@ -93,13 +102,23 @@
     return wide(lines_back, jnp.concatenate([spectrum, twisted], 0))
 
 
+def side_by_side(first, second):
+    return jnp.concatenate([first, second], 1).astype(jnp.float32)
+
+
+def packed_half(real, imag, pack_ref, half):
+    return wide(real.astype(jnp.bfloat16), pack_ref[half, 0]) + wide(
+        imag.astype(jnp.bfloat16), pack_ref[half, 1]
+    )
+
+
 def whole(shape):
     return pl.BlockSpec(shape, lambda *_: (0,) * len(shape))
 
 
 def mix_kernel(pencil_ref, lines_ref, turn_ref, part_ref, pack_ref, weight_ref, out_ref, coeff_ref, *, inner):
-    group, outs = weight_ref.shape[1], weight_ref.shape[2]
-    shape = weight_ref.shape[3:]
+    group, outs, kept, modes = weight_ref.shape[1:]
+    shape = (kept, 2 * modes)
 
     @pl.when(pl.program_id(0) == 0)
     def _():
@@ -117,19 +136,20 @@
         def one_input(i, sums):
             real, imag = coeff_ref[i, 0], coeff_ref[i, 1]
             done = []
-            for k in range(inner):
-                wr = weight_ref[0, i, first + k].astype(jnp.float32)
-                wi = weight_ref[1, i, first + k].astype(jnp.float32)
+            for k in range(inner // 2):
+                pair = first + 2 * k
+                wr = side_by_side(weight_ref[0, i, pair], weight_ref[0, i, pair + 1])
+                wi = side_by_side(weight_ref[1, i, pair], weight_ref[1, i, pair + 1])
                 done.append(sums[2 * k] + (real * wr - imag * wi))
                 done.append(sums[2 * k + 1] + (real * wi + imag * wr))
             return tuple(done)
 
         zero = jnp.zeros(shape, jnp.float32)
-        sums = lax.fori_loop(0, group, one_input, (zero,) * (2 * inner), unroll=4)
+        sums = lax.fori_loop(0, group, one_input, (zero,) * inner, unroll=2)
         for k in range(inner):
-            out_ref[first + k] = (
-                wide(sums[2 * k].astype(jnp.bfloat16), pack_ref[0])
-                + wide(sums[2 * k + 1].astype(jnp.bfloat16), pack_ref[1])
+            pair = 2 * (k // 2)
+            out_ref[first + k] = packed_half(
+                sums[pair], sums[pair + 1], pack_ref, k % 2
             ).astype(out_ref.dtype)
         return carry
 
@@ -149,11 +169,11 @@
         ],
         out_specs=[
             pl.BlockSpec((block, kept, 2 * modes), lambda s: (s, 0, 0)),
-            whole((group, 2, kept, modes)),
+            whole((group, 2, kept, 2 * modes)),
         ],
         out_shape=[
             jax.ShapeDtypeStruct((channels, kept, 2 * modes), jnp.bfloat16),
-            jax.ShapeDtypeStruct((group, 2, kept, modes), jnp.float32),
+            jax.ShapeDtypeStruct((group, 2, kept, 2 * modes), jnp.float32),
         ],
         compiler_params=params(),
         cost_estimate=pl.CostEstimate(
@@ -206,8 +226,8 @@
 
 
 def adjoint_kernel(hat_ref, lines_ref, turn_ref, part_ref, pack_ref, weight_ref, out_ref, wide_ref):
-    own, channels = weight_ref.shape[1], weight_ref.shape[2]
-    shape = weight_ref.shape[3:]
+    own, channels, kept, modes = weight_ref.shape[1:]
+    shape = (kept, 2 * modes)
 
     @pl.when(pl.program_id(0) == 0)
     def _():
@@ -221,19 +241,18 @@
     def one_output(o, sums):
         real, imag = wide_ref[o, 0], wide_ref[o, 1]
         done = []
-        for k in range(own):
-            wr = weight_ref[0, k, o].astype(jnp.float32)
-            wi = weight_ref[1, k, o].astype(jnp.float32)
-            done.append(sums[2 * k] + (real * wr + imag * wi))
-            done.append(sums[2 * k + 1] + (imag * wr - real * wi))
+        for k in range(0, own, 2):
+            wr = side_by_side(weight_ref[0, k, o], weight_ref[0, k + 1, o])
+            wi = side_by_side(weight_ref[1, k, o], weight_ref[1, k + 1, o])
+            done.append(sums[k] + (real * wr + imag * wi))
+            done.append(sums[k + 1] + (imag * wr - real * wi))
         return tuple(done)
 
     zero = jnp.zeros(shape, jnp.float32)
-    sums = lax.fori_loop(0, channels, one_output, (zero,) * (2 * own), unroll=4)
+    sums = lax.fori_loop(0, channels, one_output, (zero,) * own, unroll=4)
     for k in range(own):
-        packed = wide(sums[2 * k].astype(jnp.bfloat16), pack_ref[0]) + wide(
-            sums[2 * k + 1].astype(jnp.bfloat16), pack_ref[1]
-        )
+        pair = 2 * (k // 2)
+        packed = packed_half(sums[pair], sums[pair + 1], pack_ref, k % 2)
         values = line_values(packed.astype(jnp.bfloat16), lines_ref[...], turn_ref[...])
         out_ref[k] = values.astype(out_ref.dtype)
 
@@ -252,11 +271,11 @@
         ],
         out_specs=[
             pl.BlockSpec((block, length, 2 * modes), lambda s: (s, 0, 0)),
-            whole((channels, 2, kept, modes)),
+            whole((channels, 2, kept, 2 * modes)),
         ],
         out_shape=[
             jax.ShapeDtypeStruct((group, length, 2 * modes), jnp.bfloat16),
-            jax.ShapeDtypeStruct((channels, 2, kept, modes), jnp.float32),
+            jax.ShapeDtypeStruct((channels, 2, kept, 2 * modes), jnp.float32),
         ],
         compiler_params=params(),
         cost_estimate=pl.CostEstimate(
@@ -273,23 +292,25 @@
 
         def one_output(o, carry):
             hr, hi = hat_ref[o, 0], hat_ref[o, 1]
-            out_ref[0, i, o] = cr * hr + ci * hi
-            out_ref[1, i, o] = cr * hi - ci * hr
+            modes = out_ref.shape[-1]
+            out_ref[0, i, o] = (cr * hr + ci * hi)[:, :modes]
+            out_ref[1, i, o] = (cr * hi - ci * hr)[:, :modes]
             return carry
 
         lax.fori_loop(0, channels, one_output, 0, unroll=4)
 
 
 def outer(coeff, hat):
-    group, _, lines, modes = coeff.shape
+    group, _, lines, width = coeff.shape
+    modes = width // 2
     channels = hat.shape[0]
     block = pick(group, 2)
     return pl.pallas_call(
         outer_kernel,
         grid=(group // block,),
         in_specs=[
-            pl.BlockSpec((block, 2, lines, modes), lambda s: (s, 0, 0, 0)),
-            pl.BlockSpec((channels, 2, lines, modes), lambda s: (0, 0, 0, 0)),
+            pl.BlockSpec((block, 2, lines, width), lambda s: (s, 0, 0, 0)),
+            pl.BlockSpec((channels, 2, lines, width), lambda s: (0, 0, 0, 0)),
         ],
         out_specs=pl.BlockSpec((2, block, channels, lines, modes), lambda s: (0, s, 0, 0, 0)),
         out_shape=jax.ShapeDtypeStruct((2, group, channels, lines, modes), jnp.float32),
@@ -621,7 +642,7 @@
     lines = jnp.asarray(np.concatenate([cosine, sine], 1))
     lines_back = jnp.asarray(np.concatenate([cosine.T, sine.T], 1))
     turn, turn_back = jnp.asarray(turned(modes)), jnp.asarray(turned(modes).T)
-    part, pack = jnp.asarray(part_of(modes)), jnp.asarray(np.swapaxes(part_of(modes), 1, 2))
+    part, pack = jnp.asarray(part_of(modes)), jnp.asarray(pack_of(modes))
     slab_index = lax.axis_index("slab")
     chan_index = lax.axis_index("chan")
     weight = jnp.swapaxes(spectral_weight, 3, 4)

time: 247 us -> 256 us (1.036)
  Pallas kernels: 231 us -> 242 us
  local copies, waits for them, and re-layouts: 11 us -> 7.81 us
    pallas_call x1, Pallas kernels: 16.7 us -> 22.4 us  [adjoint_of(): pl.pallas_call(adjoint_kernel, grid=(group // block,), in_specs=[whole(ha...]
    pallas_call x1, Pallas kernels: 17.2 us -> 22.2 us  [mix(): pl.pallas_call(functools.partial(mix_kernel, inner=pick(block, 4)), grid=...]
    unnamed x25 -> x19, local copies, waits for them, and re-layouts: 3.51 us -> 0.32 us
  transfers between devices with their start and end apart: 3 -> 3, of which waited for: 0 -> 0; matrix products, arithmetic and copies ran while one was open for 1% -> 1% of each run, Pallas kernels for 22% -> 23%
where the time goes in v5:
time: 256 us; the launch traced here: 255 us
  Pallas kernels  242 us (95%)
  local copies, waits for them, and re-layouts  7.81 us (3%)
  starting transfers between devices  3.31 us (1%)
    pallas_call x6, Pallas kernels, exchange(): pl.pallas_call(functools.partial(exchange_kernel, axes, sizes, blocks), i...  138 us
    pallas_call x1, Pallas kernels, grid_stage(): pl.pallas_call(functools.partial(grid_kernel, planes=planes), grid_spec=p...  25.3 us
    pallas_call x1, Pallas kernels, adjoint_of(): pl.pallas_call(adjoint_kernel, grid=(group // block,), in_specs=[whole(ha...  22.4 us
    pallas_call x1, Pallas kernels, mix(): pl.pallas_call(functools.partial(mix_kernel, inner=pick(block, 4)), grid=...  22.2 us
    pallas_call x1, Pallas kernels, outer(): pl.pallas_call(outer_kernel, grid=(group // block,), in_specs=[pl.BlockSp...  11.7 us
    pallas_call x1, Pallas kernels, finish(): pl.pallas_call(finish_kernel, grid_spec=pltpu.PrefetchScalarGridSpec(num_...  10.6 us
    pallas_call x1, Pallas kernels, begin(): pl.pallas_call(begin_kernel, grid_spec=pltpu.PrefetchScalarGridSpec(num_s...  8.49 us
  transfers between devices with their start and end apart: 3, of which 0 were waited for; matrix products, arithmetic and copies ran while one was open for 1% of the time, Pallas kernels for 23%

profile of v5, /device:TPU:13, one launch (start us, length us, event | category | flops | bytes accessed | tf_op | source)
XLA Modules:
  0.0 255.3 jit_solution(86362848636421869)
XLA Ops:
  0.7 0.7 broadcast_in_dim.23
  1.6 8.5 %begin.1.refs_0_ = bf16[8,512,128]{2,1,0:T(8,128)(2,1)S(1)} custom-call(s32[1]{0:T(128)} %bitcast.chan_ref, bf16[64,32,4096]{2,1,0:T(8,128)(2,1)} %field_ref.3, bf16[4096,1024]{1,0:T(8,128)(2,1)} %constant.106.clone.table_ref), custom_call_target="tpu_custom_call" | custom-call | flops 4294967296 | bytes 12582912 | tf_op jit(solution)/shard_map/begin/pallas_call | solution.py:510
  10.1 27.3 %exchange.6 = bf16[8,512,128]{2,1,0:T(8,128)(2,1)S(1)} custom-call(bf16[8,512,128]{2,1,0:T(8,128)(2,1)S(1)} %begin.1.refs_0_), custom_call_target="tpu_custom_call" | custom-call | bytes 1048576 | tf_op jit(solution)/shard_map/exchange/pallas_call | solution.py:602
  37.7 22.2 %mix.1 = (bf16[64,32,128]{2,1,0:T(8,128)(2,1)S(1)}, f32[16,2,32,128]{3,2,1,0:T(8,128)S(1)}) custom-call(bf16[16,256,128]{2,1,0:T(8,128)(2,1)S(1)} %bitcast.52, bf16[32,512]{1,0:T(8,128)(2,1)S(1)} %copy-done.6, bf16[128,128]{1,0:T(8,128)(2,1)S(1)} %copy-done.5, bf16[2,128,128]{2,1,0:T(8,128)(2,1)S(1)} %copy-done.2, bf16[2,2,128,128]{3,2,1,0:T(8,128)(2,1)S(1)} %copy-done, ...), custom_call_target="tpu_custom_call" | custom-call | flops 16777216 | bytes 16777216 | tf_op jit(solution)/shard_map/mix/pallas_call | solution.py:162
  59.9 8.6 %exchange.7.parts_ref = bf16[4,16,32,128]{3,2,1,0:T(8,128)(2,1)S(1)} custom-call(bf16[4,16,32,128]{3,2,1,0:T(8,128)(2,1)S(1)} %bitcast.65), custom_call_target="tpu_custom_call" | custom-call | bytes 524288 | tf_op jit(solution)/shard_map/exchange/pallas_call | solution.py:602
  68.5 1.9 spread.1
  70.4 0.3 copy.23
  70.7 28.3 %exchange.8 = bf16[32,16,8,128]{3,2,1,0:T(8,128)(2,1)S(1)} custom-call(bf16[32,16,8,128]{3,2,1,0:T(8,128)(2,1)S(1)} %bitcast.56), custom_call_target="tpu_custom_call" | custom-call | bytes 1048576 | tf_op jit(solution)/shard_map/exchange/pallas_call | solution.py:602
  99.1 25.3 %grid.1 = (bf16[512,4096]{1,0:T(8,128)(2,1)}, bf16[8,512,128]{2,1,0:T(8,128)(2,1)S(1)}, f32[72,64]{1,0:T(8,128)S(1)}) custom-call(s32[1]{0:T(128)} %bitcast.chan_ref, bf16[512,1024]{1,0:T(8,128)(2,1)S(1)} %copy_bitcast_fusion.2.modes_ref, bf16[4096,1024]{1,0:T(8,128)(2,1)} %constant.106.clone.table_ref, bf16[64,32,4096]{2,1,0:T(8,128)(2,1)} %field_ref.3, ...), custom_call_target="tpu_custom_call" | custom-call | flops 15032385536 | bytes 20971520 | tf_op jit(solution)/shard_map/grid/pallas_call | solution.py:402
  124.5 38.4 %exchange.9 = (bf16[32,16,8,128]{3,2,1,0:T(8,128)(2,1)S(1)}, f32[32,24,64]{2,1,0:T(8,128)S(1)}) custom-call(bf16[32,16,8,128]{3,2,1,0:T(8,128)(2,1)S(1)} %bitcast.61, f32[4,24,64]{2,1,0:T(8,128)S(1)} %pad_maximum_fusion.refs_1_), custom_call_target="tpu_custom_call" | custom-call | bytes 1060864 | tf_op jit(solution)/shard_map/exchange/pallas_call | solution.py:602
  163.2 1.6 lines.1
  164.8 9.8 %exchange.10 = bf16[4,16,32,128]{3,2,1,0:T(8,128)(2,1)S(1)} custom-call(bf16[1,16,32,128]{3,2,1,0:T(8,128)(2,1)S(1)} %bitcast.64), custom_call_target="tpu_custom_call" | custom-call | bytes 131072 | tf_op jit(solution)/shard_map/exchange/pallas_call | solution.py:602
  174.6 3.9 %dynamic-slice_bitcast_fusion = (bf16[16,8,4096]{2,1,0:T(8,128)(2,1)}, bf16[16,8,4096]{2,1,0:T(8,128)(2,1)}, bf16[16,8,4096]{2,1,0:T(8,128)(2,1)}, bf16[16,8,4096]{2,1,0:T(8,128)(2,1)S(1)}) fusion(bf16[4,16,8,4096]{3,2,1,0:T(8,128)(2,1)} %bitcast.70, s32[]{:T(128)S(6)} %select_n.78, s32[]{:T(128)S(6)} %select_n.76, s32[]{:T(128)S(6)} %select_n.74, ...), kind=kLoop, calls=%fused_computation.3 | loop fusion | bytes 8388624 | tf_op jit(solution)/shard_map/jit(dynamic_index_in_dim)/squeeze | solution.py:710
  178.5 1.3 collective-permute-start.1
  179.8 2.0 collective-permute-start
  181.8 1.0 reduce_sum.9
  182.9 0.6 slice.16
  183.5 22.4 %adjoint.1 = (bf16[16,256,128]{2,1,0:T(8,128)(2,1)S(1)}, f32[64,2,32,128]{3,2,1,0:T(8,128)S(1)}) custom-call(bf16[64,32,128]{2,1,0:T(8,128)(2,1)S(1)} %bitcast.60, bf16[256,64]{1,0:T(8,128)(2,1)S(1)} %copy-done.3, bf16[128,128]{1,0:T(8,128)(2,1)S(1)} %copy-done.4, bf16[2,128,128]{2,1,0:T(8,128)(2,1)S(1)} %copy-done.2, bf16[2,2,128,128]{3,2,1,0:T(8,128)(2,1)S(1)} %copy-done, ...), custom_call_target="tpu_custom_call" | custom-call | flops 16777216 | bytes 16777216 | tf_op jit(solution)/shard_map/adjoint/pallas_call | solution.py:264
  206.0 25.5 %exchange.11 = bf16[8,16,32,128]{3,2,1,0:T(8,128)(2,1)S(1)} custom-call(bf16[8,16,32,128]{3,2,1,0:T(8,128)(2,1)S(1)} %bitcast.58), custom_call_target="tpu_custom_call" | custom-call | bytes 1048576 | tf_op jit(solution)/shard_map/exchange/pallas_call | solution.py:602
  231.5 0.7 copy.28
  232.2 0.3 copy.33
  232.5 11.7 %outer.1 = f32[2,16,64,32,64]{4,3,2,1,0:T(8,128)} custom-call(f32[16,2,32,128]{3,2,1,0:T(8,128)S(1)} %get-tuple-element.23.coeff_ref, f32[64,2,32,128]{3,2,1,0:T(8,128)S(1)} %get-tuple-element.24.hat_ref), custom_call_target="tpu_custom_call" | custom-call | flops 12582912 | bytes 33554432 | tf_op jit(solution)/shard_map/outer/pallas_call | solution.py:308
  244.1 0.5 slice_bitcast_fusion
  244.7 10.6 %finish.1 = bf16[512,4096]{1,0:T(8,128)(2,1)} custom-call(s32[1]{0:T(128)} %bitcast.chan_ref, bf16[512,1024]{1,0:T(8,128)(2,1)S(1)} %bitcast.51, bf16[4096,1024]{1,0:T(8,128)(2,1)} %constant.106.clone.table_ref, bf16[16,8,4096]{2,1,0:T(8,128)(2,1)S(1)} %get-tuple-element.29.refs_0_, bf16[16,8,4096]{2,1,0:T(8,128)(2,1)S(1)} %collective-permute-done.refs_1_, ...), custom_call_target="tpu_custom_call" | custom-call | flops 4294967296 | bytes 16777216 | tf_op jit(solution)/shard_map/finish/pallas_call | solution.py:462
  (33 shorter events, 0.8 us)
Async XLA Ops:
  1.6 36.0 %copy-start = (bf16[2,2,128,128]{3,2,1,0:T(8,128)(2,1)S(1)}, bf16[2,2,128,128]{3,2,1,0:T(8,128)(2,1)}, u32[]{:S(2)}) copy-start(bf16[2,2,128,128]{3,2,1,0:T(8,128)(2,1)} %constant.112.clone.pack_ref) | copy-start | bytes 393220
  1.6 36.0 %copy-start.2 = (bf16[2,128,128]{2,1,0:T(8,128)(2,1)S(1)}, bf16[2,128,128]{2,1,0:T(8,128)(2,1)}, u32[]{:S(2)}) copy-start(bf16[2,128,128]{2,1,0:T(8,128)(2,1)} %constant.111.clone.part_ref) | copy-start | bytes 196612
  1.6 36.0 %copy-start.5 = (bf16[128,128]{1,0:T(8,128)(2,1)S(1)}, bf16[128,128]{1,0:T(8,128)(2,1)}, u32[]{:S(2)}) copy-start(bf16[128,128]{1,0:T(8,128)(2,1)} %constant.109.clone.turn_ref) | copy-start | bytes 98308
  1.6 36.0 %copy-start.6 = (bf16[32,512]{1,0:T(8,128)(2,1)S(1)}, bf16[32,512]{1,0:T(8,128)(2,1)}, u32[]{:S(2)}) copy-start(bf16[32,512]{1,0:T(8,128)(2,1)} %constant.107.clone.lines_ref) | copy-start | bytes 98308
  37.6 30.9 %copy-start.3 = (bf16[256,64]{1,0:T(8,128)(2,1)S(1)}, bf16[256,64]{1,0:T(8,128)(2,1)}, u32[]{:S(2)}) copy-start(bf16[256,64]{1,0:T(8,128)(2,1)} %constant.108.clone.lines_ref) | copy-start | bytes 98308
  37.6 30.9 %copy-start.4 = (bf16[128,128]{1,0:T(8,128)(2,1)S(1)}, bf16[128,128]{1,0:T(8,128)(2,1)}, u32[]{:S(2)}) copy-start(bf16[128,128]{1,0:T(8,128)(2,1)} %constant.110.clone.turn_ref) | copy-start | bytes 98308
  59.9 39.2 %copy-start.7 = (bf16[64,64]{1,0:T(8,128)(2,1)S(1)}, bf16[64,64]{1,0:T(8,128)(2,1)}, u32[]{:S(2)}) copy-start(bf16[64,64]{1,0:T(8,128)(2,1)} %point_weight_ref.1) | copy-start | bytes 24580
  59.9 39.2 %copy-start.8 = (bf16[512,64]{1,0:T(8,128)(2,1)S(1)}, bf16[512,64]{1,0:T(8,128)(2,1)}, u32[]{:S(2)}) copy-start(bf16[512,64]{1,0:T(8,128)(2,1)} %constant.113.clone.repeat_ref) | copy-start | bytes 196612
  162.9 11.7 %copy-start.1 = (f32[32,24,64]{2,1,0:T(8,128)}, f32[32,24,64]{2,1,0:T(8,128)S(1)}, u32[]{:S(2)}) copy-start(f32[32,24,64]{2,1,0:T(8,128)S(1)} %get-tuple-element.25) | copy-start | bytes 589828
  178.5 66.2 %collective-permute-start.2 = (bf16[16,8,4096]{2,1,0:T(8,128)(2,1)}, bf16[16,8,4096]{2,1,0:T(8,128)(2,1)}, u32[]{:S(2)}, u32[]{:S(2)}) collective-permute-start(bf16[16,8,4096]{2,1,0:T(8,128)(2,1)} %get-tuple-element.26), channel_id=1, source_target_pairs={{0,3},{1,0},{2,1},{3,2},{4,7},{5,4},{6,5},{7,6},{8,11},{9,8},{10,9... | collective-permute-start | bytes 3145736 | tf_op jit(solution)/shard_map/ppermute | solution.py:712
  178.5 66.2 %collective-permute-start.1 = (bf16[16,8,4096]{2,1,0:T(8,128)(2,1)}, bf16[16,8,4096]{2,1,0:T(8,128)(2,1)}, u32[]{:S(2)}, u32[]{:S(2)}) collective-permute-start(bf16[16,8,4096]{2,1,0:T(8,128)(2,1)} %get-tuple-element.27), channel_id=1, source_target_pairs={{0,2},{1,3},{2,0},{3,1},{4,6},{5,7},{6,4},{7,5},{8,10},{9,11},{10,... | collective-permute-start | bytes 3145736 | tf_op jit(solution)/shard_map/ppermute | solution.py:712
  179.8 64.8 %collective-permute-start = (bf16[16,8,4096]{2,1,0:T(8,128)(2,1)}, bf16[16,8,4096]{2,1,0:T(8,128)(2,1)S(1)}, u32[]{:S(2)}, u32[]{:S(2)}) collective-permute-start(bf16[16,8,4096]{2,1,0:T(8,128)(2,1)} %get-tuple-element.28), channel_id=1, source_target_pairs={{0,1},{1,2},{2,3},{3,0},{4,5},{5,6},{6,7},{7,4},{8,9},{9,10},{10,1... | collective-permute-start | bytes 3145736 | tf_op jit(solution)/shard_map/ppermute | solution.py:712
